TPU v7x, 256 devices: a whole 4x4x8 slice. The times are simulated.
256 devices in a mesh: seq: 64 (over x, y, z_lo), mp: 4 (over z_hi, core).
Axes of the slice: x: 4, y: 4, z: 8 (z_hi: 2, z_lo: 4; z = z_hi * 4 + z_lo), core: 2. Of those that a mesh axis runs over, the one named last changes fastest.
Arguments:
- activations: bfloat16 [16384, 1536], P('seq', 'mp'), may hold values from -48 to 48
- proj_weight: bfloat16 [3, 1536, 1536], P(None, None, 'mp'), may hold values from -0.15625 to 0.15625
- out_grad: bfloat16 [16384, 1536], P('seq', 'mp'), may hold values from -6 to 6
- neighbours: int32 [128, 9], replicated, may hold values from 0 to 127, as said below
Outputs:
- attn_out: bfloat16 [16384, 1536], P('seq', 'mp')
- grad_input: bfloat16 [16384, 1536], P('seq', 'mp')
- grad_weight: float32 [3, 1536, 1536], P(None, 'seq', 'mp')
Inputs may be any that keep to these rules, and one draw needn't show every extreme that they name: `neighbours`: row b names 9 different blocks and its first entry is b itself. Block g lies in shard g // 2; every entry g of row b satisfies (g // 2 - b // 2) mod (64) <= 2 or >= 62.
All inputs are finite; a program needn't handle non-finite values.
Results may differ from a plain program's by a relative error of at most 0.022.
Values may be sent and summed in bfloat16 or wider, within the bound.
No kernel may reach another device: no remote copies, remote signals or barrier semaphores. Data moves between devices by JAX's collectives and lax.ppermute only.
A program may use at most 128 MiB of HBM per device.

v0:
```python
import math

import jax
import jax.numpy as jnp
from jax import lax
from jax.experimental import pallas as pl
from jax.experimental.pallas import tpu as pltpu
from jax.sharding import PartitionSpec as P

HD = 128
BLK = 128
REACH = 2
SLABS = 2 * REACH + 1
SIDE = 4
SEQ = SIDE**3
AXES = ("seq", "mp")
F32 = jnp.float32
BF16 = jnp.bfloat16
OFF = -1e30


def flat(x, y, z, h, c):
    return (((x * SIDE + y) * SIDE + z) * 2 + h) * 2 + c


def coords(i):
    return i // 64, i // 16 % 4, i // 4 % 4, i // 2 % 2, i % 2


def move(value, to):
    return lax.ppermute(value, AXES, [(i, flat(*to(*coords(i)))) for i in range(256)])


def turned(y, z):
    return jnp.where(y % 2 == 1, 3 - z, z) if isinstance(y, jax.Array) else (3 - z if y % 2 else z)


def shard_at(x, y, z):
    return (x * SIDE + y) * SIDE + turned(y, z)


def place_of(s):
    x, y, z = s // 16, s // 4 % 4, s % 4
    return x, y, turned(y, z)


def along_chain(value, steps):
    def to(x, y, z, h, c):
        return (*place_of((shard_at(x, y, z) + steps) % SEQ), h, c)

    return move(value, to)


def reversal(value):
    return move(value, lambda x, y, z, h, c: (x, y, turned(y, z), h, c))


NT = (((1,), (1,)), ((), ()))
NN = (((1,), (0,)), ((), ()))
TN = (((0,), (0,)), ((), ()))


def dot(a, b, dims):
    return lax.dot_general(a, b, dims, preferred_element_type=F32)


def attention_kernel(q_ref, do_ref, bias_ref, *refs):
    kv = refs[:SLABS]
    out_ref, dq_ref, own_ref = refs[SLABS : SLABS + 3]
    grads = refs[SLABS + 3 :]
    inv_root = 1.0 / math.sqrt(HD)
    width = q_ref.shape[1]
    for head in range(width // HD):
        cols = pl.ds(head * HD, HD)
        late = pl.ds(width + head * HD, HD)
        q = q_ref[:, cols]
        do = do_ref[:, cols]
        raw = []
        for w in range(SLABS):
            s = dot(kv[w][:, cols], q, NT) * inv_root
            top = s[:BLK] + bias_ref[2 * w : 2 * w + 1, :]
            low = s[BLK:] + bias_ref[2 * w + 1 : 2 * w + 2, :]
            raw.append(jnp.concatenate([top, low], axis=0))
        peak = raw[0].max(axis=0, keepdims=True)
        for s in raw[1:]:
            peak = jnp.maximum(peak, s.max(axis=0, keepdims=True))
        grown = [jnp.exp(s - peak) for s in raw]
        total = sum(e.sum(axis=0, keepdims=True) for e in grown)
        scale = 1.0 / total
        prob = [e * scale for e in grown]
        prob_b = [p.astype(BF16) for p in prob]
        out_t = sum(dot(kv[w][:, late], prob_b[w], TN) for w in range(SLABS))
        out = out_t.T.astype(BF16)
        out_ref[:, cols] = out
        delta = jnp.sum(do.astype(F32) * out.astype(F32), axis=1, keepdims=True)
        delta_t = jnp.broadcast_to(delta, (delta.shape[0], HD)).T[0:1, :]
        dq_t = None
        for w in range(SLABS):
            dp = dot(kv[w][:, late], do, NT)
            ds = (prob[w] * (dp - delta_t) * inv_root).astype(BF16)
            term = dot(kv[w][:, cols], ds, TN)
            dq_t = term if dq_t is None else dq_t + term
            dk = dot(ds, q, NN)
            dv = dot(prob_b[w], do, NN)
            if w == REACH:
                own_ref[:, cols] = dk
                own_ref[:, late] = dv
            grads[w][:, cols] = dk.astype(BF16)
            grads[w][:, late] = dv.astype(BF16)
        dq_ref[:, cols] = dq_t.T.astype(BF16)


def attention(queries, out_grad, bias, slabs):
    rows, width = queries.shape
    return pl.pallas_call(
        attention_kernel,
        out_shape=[
            jax.ShapeDtypeStruct((rows, width), BF16),
            jax.ShapeDtypeStruct((rows, width), BF16),
            jax.ShapeDtypeStruct((rows, 2 * width), F32),
        ]
        + [jax.ShapeDtypeStruct((rows, 2 * width), BF16)] * SLABS,
        in_specs=[pl.BlockSpec(memory_space=pltpu.VMEM)] * (3 + SLABS),
        out_specs=[pl.BlockSpec(memory_space=pltpu.VMEM)] * (3 + SLABS),
        compiler_params=pltpu.CompilerParams(vmem_limit_bytes=40 * 1024 * 1024),
        cost_estimate=pl.CostEstimate(
            flops=12 * rows * SLABS * rows * width,
            bytes_accessed=20 * rows * width * 2,
            transcendentals=SLABS * rows * rows * width // HD,
        ),
    )(queries, out_grad, bias, *slabs)


def pick(array, index, axis=0):
    return lax.dynamic_index_in_dim(array, index, axis, keepdims=False)


VMEM = pl.BlockSpec(memory_space=pltpu.VMEM)
SMEM = pl.BlockSpec(memory_space=pltpu.SMEM)
ROOMY = pltpu.CompilerParams(vmem_limit_bytes=48 * 1024 * 1024)
NB = 2 * REACH
EDGE = 96


def weight_kernel(order_ref, dq_ref, *refs):
    tokens, grads = refs[:SLABS], refs[SLABS : 2 * SLABS]
    outs, held = refs[2 * SLABS : -1], refs[-1]
    width = dq_ref.shape[1]
    deep = tokens[0].shape[1] // SIDE
    for i in range(SIDE):
        rows = pl.ds(i * deep, deep)
        held[rows, :width] = dot(tokens[REACH][:, rows], dq_ref[...], TN).astype(BF16)
        total = dot(tokens[0][:, rows], grads[0][...], TN)
        for w in range(1, SLABS):
            total = total + dot(tokens[w][:, rows], grads[w][...], TN)
        held[rows, width:] = total.astype(BF16)
    half = EDGE // 2
    for side in range(2):
        for k in range(4):
            into = outs[2 * side + k // 2]
            chunk = order_ref[side, k]
            for j in range(SIDE):
                cell = j * SIDE + chunk if side else chunk * SIDE + j
                at = pl.multiple_of(cell * EDGE + side * half, half)
                into[k % 2, j] = held[pl.ds(at, half), :]


def weight_terms(order, grad_query, tokens, grads):
    shape = (2, SIDE, EDGE // 2, 3 * grad_query.shape[1])
    depth = tokens[0].shape[1]
    return pl.pallas_call(
        weight_kernel,
        out_shape=[jax.ShapeDtypeStruct(shape, BF16)] * 4,
        in_specs=[SMEM] + [VMEM] * (1 + 2 * SLABS),
        out_specs=[VMEM] * 4,
        scratch_shapes=[pltpu.VMEM((depth, 3 * grad_query.shape[1]), BF16)],
        compiler_params=ROOMY,
        cost_estimate=pl.CostEstimate(
            flops=3_300_000_000, bytes_accessed=30_000_000, transcendentals=0
        ),
    )(order, grad_query, *tokens, *grads)


def first_sums_kernel(*refs):
    kept, got, sent, mine = refs[:2], refs[2:4], refs[4:6], refs[6:]
    for n in range(2):
        sent[n][...] = (kept[n][1].astype(F32) + got[n][1].astype(F32)).astype(BF16)
        mine[n][...] = kept[n][0].astype(F32) + got[n][0].astype(F32)


def first_sums(kept, got):
    return pl.pallas_call(
        first_sums_kernel,
        out_shape=[jax.ShapeDtypeStruct(k.shape[1:], BF16) for k in kept]
        + [jax.ShapeDtypeStruct(k.shape[1:], F32) for k in kept],
        in_specs=[VMEM] * 4,
        out_specs=[VMEM] * 4,
        compiler_params=ROOMY,
    )(*kept, *got)


def second_sums_kernel(order_ref, *refs):
    mine, got, sent, kept = refs[:2], refs[2:4], refs[4:6], refs[6:]
    for n in range(2):
        for k in range(4):
            chunk = order_ref[1 - n, k]
            value = mine[n][chunk] + got[n][chunk].astype(F32)
            if k < 2:
                sent[n][k] = value.astype(BF16)
            else:
                kept[n][k - 2] = value


def second_sums(order, mine, got):
    shape = (2, *mine[0].shape[1:])
    return pl.pallas_call(
        second_sums_kernel,
        out_shape=[jax.ShapeDtypeStruct(shape, BF16)] * 2 + [jax.ShapeDtypeStruct(shape, F32)] * 2,
        in_specs=[SMEM] + [VMEM] * 4,
        out_specs=[VMEM] * 4,
        compiler_params=ROOMY,
    )(order, *mine, *got)


def input_kernel(place_ref, dq_ref, own_ref, weight_ref, *refs):
    halo, (sent_ref, kept_ref) = refs[:2], refs[2:]
    width = dq_ref.shape[1]
    total = own_ref[...]
    for piece in halo:
        total = total + piece[...].astype(F32)
    total = total.astype(BF16)
    dk, dv, dq = total[:, :width], total[:, width:], dq_ref[...]
    for k in range(4):
        rows = pl.ds(pl.multiple_of(place_ref[k] * width, width), width)
        part = dot(dq, weight_ref[0, rows], NT)
        part = part + dot(dk, weight_ref[1, rows], NT)
        part = part + dot(dv, weight_ref[2, rows], NT)
        if k < 2:
            sent_ref[k] = part.astype(BF16)
        else:
            kept_ref[k - 2] = part


def input_terms(place, grad_query, own, proj_weight, halo):
    rows, width = grad_query.shape
    return pl.pallas_call(
        input_kernel,
        out_shape=[
            jax.ShapeDtypeStruct((2, rows, width), BF16),
            jax.ShapeDtypeStruct((2, rows, width), F32),
        ],
        in_specs=[SMEM] + [VMEM] * 5,
        out_specs=[VMEM] * 2,
        compiler_params=ROOMY,
    )(place, grad_query, own, proj_weight, *halo)


def exchanged(chunks, axis, here):
    total = pick(chunks, here)
    for step in (1, 2, 3):

        def to(*at, step=step):
            at = list(at)
            at[axis] = (at[axis] + step) % SIDE
            return tuple(at)

        sent = pick(chunks, (here + step) % SIDE).astype(BF16)
        total = total + move(sent, to).astype(F32)
    return total


def flip(i):
    return i ^ 1


def wrap(i):
    return 3 - i


def partner(axis, rule):
    def to(*at):
        at = list(at)
        at[axis] = rule(at[axis])
        return tuple(at)

    return to


def onward(axis, step):
    return partner(axis, lambda i: (i + step) % SIDE)


def swapped(value):
    return move(value, lambda x, y, z, h, c: (x, y, z, h, 1 - c))


def local(activations, proj_weight, out_grad, neighbours):
    rows, width = activations.shape
    seq, mp = lax.axis_index("seq"), lax.axis_index("mp")
    x, y, z = seq // 16, seq // 4 % 4, seq % 4
    h, c = mp // 2, mp % 2
    shard = shard_at(x, y, z)
    weight_q = proj_weight[0]
    weight_kv = jnp.concatenate([proj_weight[1], proj_weight[2]], axis=-1)

    near = reversal(activations)
    far = move(activations, lambda x, y, z, h, c: (x, y, turned(y, z), 1 - h, c))
    pair = jnp.concatenate([jnp.where(h == 0, near, far), jnp.where(h == 0, far, near)], axis=1)

    def full(mine, theirs):
        even, odd = jnp.where(c == 0, mine, theirs), jnp.where(c == 0, theirs, mine)
        return jnp.concatenate(
            [even[..., :width], odd[..., :width], even[..., width:], odd[..., width:]], axis=-1
        )

    def keys_values(tokens):
        return dot(tokens, weight_kv, NN).astype(BF16)

    mine = [None, along_chain(pair, 1), pair, along_chain(pair, -1), None]
    mine[0], mine[4] = along_chain(mine[1], 1), along_chain(mine[3], -1)
    tokens = [full(v, swapped(v)) for v in mine]
    whole = tokens[REACH]
    queries = dot(whole, weight_q, NN).astype(BF16)
    slabs = [keys_values(t) for t in tokens]
    grad_out = reversal(out_grad)

    lists = lax.dynamic_slice_in_dim(neighbours, shard * 2, 2, 0)
    window = (shard * 2 - 2 * REACH + jnp.arange(2 * SLABS)) % (2 * SEQ)
    named = jnp.any(lists[:, None, :] == window[None, :, None], axis=-1)
    bias = jnp.repeat(jnp.where(named, 0.0, OFF).astype(F32).T, BLK, axis=1)

    attended, grad_query, own, *grads = attention(queries, grad_out, bias, slabs)
    halo = []
    for far_piece, piece, way in ((grads[0], grads[1], -1), (grads[4], grads[3], 1)):
        passed = along_chain(far_piece, way).astype(F32) + piece.astype(F32)
        halo.append(along_chain(passed.astype(BF16), way))

    order = jnp.stack(
        [jnp.stack([flip(i), wrap(flip(i)), i, wrap(i)]) for i in (x, y)]
    ).astype(jnp.int32)
    sent_x, kept_x, sent_y, kept_y = weight_terms(order, grad_query, tokens, grads)
    got = [move(sent_x, partner(0, flip)), move(sent_y, partner(1, flip))]
    pass_x, pass_y, *sums = first_sums((kept_x, kept_y), got)
    pass_one = pass_x
    got = [move(pass_x, partner(0, wrap)), move(pass_y, partner(1, wrap))]
    sent_x, sent_y, kept_x, kept_y = second_sums(order, sums, got)
    got_x, got_y = move(sent_x, partner(1, flip)), move(sent_y, partner(0, flip))
    place = jnp.stack([1 - c, 3 - c, c, 2 + c]).astype(jnp.int32)
    halo = lax.optimization_barrier((pass_one, *halo))[1:]
    sent, kept = input_terms(place, grad_query, own, proj_weight, halo)
    crossed = swapped(sent)

    summed = (kept + crossed.astype(F32)).astype(BF16)
    home_far = move(pick(summed, 1 - h), lambda x, y, z, h, c: (x, y, turned(y, z), 1 - h, c))
    attn_out, home_near = reversal(jnp.stack([attended, pick(summed, h)]))
    pass_x = (kept_x[1] + got_x[1].astype(F32)).astype(BF16)
    pass_y = (kept_y[1] + got_y[1].astype(F32)).astype(BF16)
    pass_x, pass_y, home_far = lax.optimization_barrier((pass_x, pass_y, home_far))
    keep_x = kept_x[0] + got_x[0].astype(F32) + move(pass_x, partner(1, wrap)).astype(F32)
    keep_y = kept_y[0] + got_y[0].astype(F32) + move(pass_y, partner(0, wrap)).astype(F32)

    chunks = jnp.concatenate([keep_x, keep_y], axis=0).reshape(SIDE, 24, 3 * width)
    mine = exchanged(chunks, 2, z)
    grad_weight = jnp.stack([mine[:, i * width : (i + 1) * width] for i in range(3)])
    grad_input = (home_near.astype(F32) + home_far.astype(F32)).astype(BF16)
    return (attn_out, grad_input, grad_weight)


def solution(mesh):
    placed = (P("seq", "mp"), P(None, None, "mp"), P("seq", "mp"), P())
    return jax.shard_map(
        local,
        mesh=mesh,
        in_specs=placed,
        out_specs=(P("seq", "mp"), P("seq", "mp"), P(None, "seq", "mp")),
        check_vma=False,
    )
```

profile of v0, /device:TPU:24, one launch (start us, length us, event | category | flops | bytes accessed | tf_op | source)
XLA Modules:
  0.0 150.7 jit_solution(17946417293293911072)
XLA Ops:
  0.6 6.5 %collective-permute-start = (bf16[256,384]{1,0:T(8,128)(2,1)}, bf16[256,384]{1,0:T(8,128)(2,1)S(1)}, u32[]{:S(2)}, u32[]{:S(2)}) collective-permute-start(bf16[256,384]{1,0:T(8,128)(2,1)} %param.4), channel_id=1, source_target_pairs={{0,0},{1,1},{2,2},{3,3},{4,4},{5,5},{6,6},{7,7},{8,8},{9,9},{10,10... | collective-permute-start | bytes 589832 | tf_op jit(solution)/shard_map/ppermute | solution.py:31
  7.2 3.2 %collective-permute-start.1 = (bf16[256,384]{1,0:T(8,128)(2,1)}, bf16[256,384]{1,0:T(8,128)(2,1)S(1)}, u32[]{:S(2)}, u32[]{:S(2)}) collective-permute-start(bf16[256,384]{1,0:T(8,128)(2,1)} %param.4), channel_id=1, source_target_pairs={{0,2},{1,3},{2,0},{3,1},{4,6},{5,7},{6,4},{7,5},{8,10},{9,11},{10,... | collective-permute-start | bytes 589832 | tf_op jit(solution)/shard_map/ppermute | solution.py:31
  10.4 3.8 %collective-permute-start.3 = (bf16[256,384]{1,0:T(8,128)(2,1)}, bf16[256,384]{1,0:T(8,128)(2,1)S(1)}, u32[]{:S(2)}, u32[]{:S(2)}) collective-permute-start(bf16[256,384]{1,0:T(8,128)(2,1)} %param.6), channel_id=1, source_target_pairs={{0,0},{1,1},{2,2},{3,3},{4,4},{5,5},{6,6},{7,7},{8,8},{9,9},{10,10... | collective-permute-start | bytes 589832 | tf_op jit(solution)/shard_map/ppermute | solution.py:31
  14.4 0.1 copy.8
  14.5 0.2 compare_reduce_fusion
  14.7 0.1 copy.9
  15.0 3.8 %collective-permute-done.1 = bf16[256,384]{1,0:T(8,128)(2,1)S(1)} collective-permute-done((bf16[256,384]{1,0:T(8,128)(2,1)}, bf16[256,384]{1,0:T(8,128)(2,1)S(1)}, u32[]{:S(2)}, u32[]{:S(2)}) %collective-permute-start.1) | collective-permute-done | bytes 196640 | tf_op jit(solution)/shard_map/ppermute | solution.py:31
  18.9 3.7 %collective-permute-start.8 = (bf16[256,768]{1,0:T(8,128)(2,1)S(1)}, bf16[256,768]{1,0:T(8,128)(2,1)S(1)}, u32[]{:S(2)}, u32[]{:S(2)}) collective-permute-start(bf16[256,768]{1,0:T(8,128)(2,1)S(1)} %pad_maximum_fusion.7), channel_id=1, source_target_pairs={{0,240},{1,241},{2,242},{3,243},{4,0},{5,1},{6,2},{7,3},{8,4},{9,5... | collective-permute-start | bytes 1179656 | tf_op jit(solution)/shard_map/ppermute | solution.py:31
  22.6 1.9 %slice_bitcast_fusion.1 = (bf16[1536,384]{1,0:T(8,128)(2,1)S(1)}, bf16[1536,384]{1,0:T(8,128)(2,1)S(1)}) fusion(bf16[3,1536,384]{2,1,0:T(8,128)(2,1)} %weight_ref.1), kind=kLoop, calls=%fused_computation.9 | loop fusion | bytes 4718592 | tf_op jit(solution)/shard_map/squeeze | solution.py:304
  24.5 0.6 collective-permute-start.4
  25.1 6.6 %collective-permute-done.8 = bf16[256,768]{1,0:T(8,128)(2,1)S(1)} collective-permute-done((bf16[256,768]{1,0:T(8,128)(2,1)S(1)}, bf16[256,768]{1,0:T(8,128)(2,1)S(1)}, u32[]{:S(2)}, u32[]{:S(2)}) %collective-permute-start.8) | collective-permute-done | bytes 393248 | tf_op jit(solution)/shard_map/ppermute | solution.py:31
  31.7 0.1 collective-permute-start.10
  31.8 0.1 broadcast_select_fusion.9
  32.1 4.0 %collective-permute-done.4 = bf16[256,768]{1,0:T(8,128)(2,1)S(1)} collective-permute-done((bf16[256,768]{1,0:T(8,128)(2,1)S(1)}, bf16[256,768]{1,0:T(8,128)(2,1)S(1)}, u32[]{:S(2)}, u32[]{:S(2)}) %collective-permute-start.4) | collective-permute-done | bytes 393248 | tf_op jit(solution)/shard_map/ppermute | solution.py:31
  36.1 2.6 %collective-permute-start.5 = (bf16[256,768]{1,0:T(8,128)(2,1)S(1)}, bf16[256,768]{1,0:T(8,128)(2,1)S(1)}, u32[]{:S(2)}, u32[]{:S(2)}) collective-permute-start(bf16[256,768]{1,0:T(8,128)(2,1)S(1)} %collective-permute-done.4), channel_id=1, source_target_pairs={{0,4},{1,5},{2,6},{3,7},{4,8},{5,9},{6,10},{7,11},{8,12},{9,13},{1... | collective-permute-start | bytes 1179656 | tf_op jit(solution)/shard_map/ppermute | solution.py:31
  38.7 0.8 convolution_convert_fusion.2.refs_2_
  39.5 1.9 %fusion.3.q_ref = bf16[256,384]{1,0:T(8,128)(2,1)S(1)} fusion(bf16[3,1536,384]{2,1,0:T(8,128)(2,1)} %weight_ref.1, bf16[256,384]{1,0:T(8,128)(2,1)S(1)} %get-tuple-element.101, bf16[256,384]{1,0:T(8,128)(2,1)S(1)} %get-tuple-element.91, bf16[256,384]{1,0:T(8,128)(2,1)S(1)} %get-tuple-element.102, bf16[256,384]{1,0:T(8,128)(2,1)S(1)} %get-tuple-element.90), kind=kOutput, calls=%fused_computation.11 | convolution fusion | flops 305233920 | bytes 2162688 | tf_op jit(solution)/shard_map/dot_general | solution.py:64
  41.3 2.2 %collective-permute-done.10 = bf16[256,768]{1,0:T(8,128)(2,1)S(1)} collective-permute-done((bf16[256,768]{1,0:T(8,128)(2,1)S(1)}, bf16[256,768]{1,0:T(8,128)(2,1)S(1)}, u32[]{:S(2)}, u32[]{:S(2)}) %collective-permute-start.10) | collective-permute-done | bytes 393248 | tf_op jit(solution)/shard_map/ppermute | solution.py:31
  43.8 0.1 broadcast_select_fusion.5
  43.9 0.8 convolution_convert_fusion.1.refs_3_
  44.7 0.1 fusion.19
  44.8 3.0 %collective-permute-done.5 = bf16[256,768]{1,0:T(8,128)(2,1)S(1)} collective-permute-done((bf16[256,768]{1,0:T(8,128)(2,1)S(1)}, bf16[256,768]{1,0:T(8,128)(2,1)S(1)}, u32[]{:S(2)}, u32[]{:S(2)}) %collective-permute-start.5) | collective-permute-done | bytes 393248 | tf_op jit(solution)/shard_map/ppermute | solution.py:31
  47.7 0.8 convolution_convert_fusion.3.refs_1_
  48.6 0.1 broadcast_select_fusion.1
  48.7 0.1 fusion.15
  48.9 0.8 convolution_convert_fusion.refs_4_
  50.0 0.8 convolution_convert_fusion.4.refs_0_
  50.8 6.2 %shard_map.67 = (bf16[256,384]{1,0:T(8,128)(2,1)S(1)}, bf16[256,384]{1,0:T(8,128)(2,1)S(1)}, f32[256,768]{1,0:T(8,128)S(1)}, bf16[256,768]{1,0:T(8,128)(2,1)S(1)...) custom-call(bf16[256,384]{1,0:T(8,128)(2,1)S(1)} %fusion.3.q_ref, ...), custom_call_target="tpu_custom_call" | custom-call | flops 1509949440 | bytes 3932160 | tf_op jit(solution)/shard_map/pallas_call | solution.py:115
  57.0 0.9 copy-done.7
  57.9 0.7 copy-done.11
  58.6 4.6 %collective-permute-start.16 = (bf16[256,768]{1,0:T(8,128)(2,1)S(1)}, bf16[256,768]{1,0:T(8,128)(2,1)S(1)}, u32[]{:S(2)}, u32[]{:S(2)}) collective-permute-start(bf16[256,768]{1,0:T(8,128)(2,1)S(1)} %get-tuple-element.37.refs_9_), channel_id=1, source_target_pairs={{0,4},{1,5},{2,6},{3,7},{4,8},{5,9},{6,10},{7,11},{8,12},{9,13},{1... | collective-permute-start | bytes 1179656 | tf_op jit(solution)/shard_map/ppermute | solution.py:31
  63.2 6.1 %shard_map.68 = (bf16[2,4,48,1152]{3,2,1,0:T(8,128)(2,1)}, bf16[2,4,48,1152]{3,2,1,0:T(8,128)(2,1)}, bf16[2,4,48,1152]{3,2,1,0:T(8,128)(2,1)}, bf16[2,4,48,1152]{3,2,1,0:T(8,128)(2,1)}) custom-call(s32[2,4]{1,0:T(2,128)S(1)} %pad_add_fusion.order_ref, bf16[256,384]{1,0:T(8,128)(2,1)S(1)} %get-tuple-element.31.dq_ref, ...), custom_call_target="tpu_custom_call" | custom-call | flops 3300000000 | bytes 30000000 | tf_op jit(solution)/shard_map/pallas_call | solution.py:171
  69.3 1.6 %collective-permute-start.12 = (bf16[2,4,48,1152]{3,2,1,0:T(8,128)(2,1)}, bf16[2,4,48,1152]{3,2,1,0:T(8,128)(2,1)S(1)}, u32[]{:S(2)}, u32[]{:S(2)}) collective-permute-start(bf16[2,4,48,1152]{3,2,1,0:T(8,128)(2,1)} %get-tuple-element.40), channel_id=1, source_target_pairs={{0,64},{1,65},{2,66},{3,67},{4,68},{5,69},{6,70},{7,71},{8,72},{9,... | collective-permute-start | bytes 2654216 | tf_op jit(solution)/shard_map/ppermute | solution.py:31
  70.8 1.7 %collective-permute-done.16 = bf16[256,768]{1,0:T(8,128)(2,1)S(1)} collective-permute-done((bf16[256,768]{1,0:T(8,128)(2,1)S(1)}, bf16[256,768]{1,0:T(8,128)(2,1)S(1)}, u32[]{:S(2)}, u32[]{:S(2)}) %collective-permute-start.16) | collective-permute-done | bytes 393248 | tf_op jit(solution)/shard_map/ppermute | solution.py:31
  72.6 0.8 add_convert_fusion.1
  73.4 7.3 %collective-permute-start.17 = (bf16[256,768]{1,0:T(8,128)(2,1)}, bf16[256,768]{1,0:T(8,128)(2,1)}, u32[]{:S(2)}, u32[]{:S(2)}) collective-permute-start(bf16[256,768]{1,0:T(8,128)(2,1)} %add_convert_fusion.1), channel_id=1, source_target_pairs={{0,4},{1,5},{2,6},{3,7},{4,8},{5,9},{6,10},{7,11},{8,12},{9,13},{1... | collective-permute-start | bytes 1179656 | tf_op jit(solution)/shard_map/ppermute | solution.py:31
  80.7 0.9 add_convert_fusion.2
  81.6 10.1 %collective-permute-done.12.refs_2_ = bf16[2,4,48,1152]{3,2,1,0:T(8,128)(2,1)S(1)} collective-permute-done((bf16[2,4,48,1152]{3,2,1,0:T(8,128)(2,1)}, bf16[2,4,48,1152]{3,2,1,0:T(8,128)(2,1)S(1)}, u32[]{:S(2)}, u32[]{:S(2)}) %collective-permute-start.12) | collective-permute-done | bytes 884768 | tf_op jit(solution)/shard_map/ppermute | solution.py:31
  91.7 0.9 collective-permute-done.13.refs_3_
  92.6 1.2 shard_map.69
  93.8 0.9 copy-done.5
  94.7 5.9 %collective-permute-start.20 = (bf16[4,48,1152]{2,1,0:T(8,128)(2,1)}, bf16[4,48,1152]{2,1,0:T(8,128)(2,1)S(1)}, u32[]{:S(2)}, u32[]{:S(2)}) collective-permute-start(bf16[4,48,1152]{2,1,0:T(8,128)(2,1)} %get-tuple-element.42), channel_id=1, source_target_pairs={{0,192},{1,193},{2,194},{3,195},{4,196},{5,197},{6,198},{7,199},{8... | collective-permute-start | bytes 1327112 | tf_op jit(solution)/shard_map/ppermute | solution.py:31
  100.6 2.7 %collective-permute-start.21 = (bf16[4,48,1152]{2,1,0:T(8,128)(2,1)}, bf16[4,48,1152]{2,1,0:T(8,128)(2,1)S(1)}, u32[]{:S(2)}, u32[]{:S(2)}) collective-permute-start(bf16[4,48,1152]{2,1,0:T(8,128)(2,1)} %get-tuple-element.49), channel_id=1, source_target_pairs={{0,48},{1,49},{2,50},{3,51},{4,52},{5,53},{6,54},{7,55},{8,56},{9,... | collective-permute-start | bytes 1327112 | tf_op jit(solution)/shard_map/ppermute | solution.py:31
  103.4 4.8 %collective-permute-done.15.refs_0_ = bf16[256,768]{1,0:T(8,128)(2,1)} collective-permute-done((bf16[256,768]{1,0:T(8,128)(2,1)}, bf16[256,768]{1,0:T(8,128)(2,1)}, u32[]{:S(2)}, u32[]{:S(2)}) %collective-permute-start.15) | collective-permute-done | bytes 393248 | tf_op jit(solution)/shard_map/ppermute | solution.py:31
  108.2 4.0 %shard_map.70 = (bf16[2,256,384]{2,1,0:T(8,128)(2,1)S(1)}, f32[2,256,384]{2,1,0:T(8,128)S(1)}) custom-call(s32[4]{0:T(128)S(1)} %pad_add_fusion.1.place_ref, bf16[256,384]{1,0:T(8,128)(2,1)S(1)} %copy-done.10, f32[256,768]{1,0:T(8,128)S(1)} %copy-done.8, bf16[3,1536,384]{2,1,0:T(8,128)(2,1)} %weight_ref.1, bf16[256,768]{1,0:T(8,128)(2,1)} %collective-permute-done.15.refs_0_, ...), custom_call_target="tpu_custom_call" | custom-call | tf_op jit(solution)/shard_map/pallas_call | solution.py:246
  112.3 0.1 collective-permute-start.18
  112.4 5.0 %collective-permute-done.21.refs_3_ = bf16[4,48,1152]{2,1,0:T(8,128)(2,1)S(1)} collective-permute-done((bf16[4,48,1152]{2,1,0:T(8,128)(2,1)}, bf16[4,48,1152]{2,1,0:T(8,128)(2,1)S(1)}, u32[]{:S(2)}, u32[]{:S(2)}) %collective-permute-start.21) | collective-permute-done | bytes 442400 | tf_op jit(solution)/shard_map/ppermute | solution.py:31
  117.5 1.2 copy-done.4
  118.6 0.7 shard_map.71
  119.5 1.1 add_convert_fusion
  120.8 0.6 collective-permute-start.22
  121.4 5.4 %collective-permute-done.23 = bf16[2,48,1152]{2,1,0:T(8,128)(2,1)S(1)} collective-permute-done((bf16[2,48,1152]{2,1,0:T(8,128)(2,1)S(1)}, bf16[2,48,1152]{2,1,0:T(8,128)(2,1)S(1)}, u32[]{:S(2)}, u32[]{:S(2)}) %collective-permute-start.23) | collective-permute-done | bytes 221216 | tf_op jit(solution)/shard_map/ppermute | solution.py:31
  126.8 1.4 collective-permute-done.22
  128.2 0.6 collective-permute-done.24
  128.8 3.8 %collective-permute-start.25 = (bf16[48,1152]{1,0:T(8,128)(2,1)S(1)}, bf16[48,1152]{1,0:T(8,128)(2,1)S(1)}, u32[]{:S(2)}, u32[]{:S(2)}) collective-permute-start(bf16[48,1152]{1,0:T(8,128)(2,1)S(1)} %fusion.7), channel_id=1, source_target_pairs={{0,48},{1,49},{2,50},{3,51},{4,52},{5,53},{6,54},{7,55},{8,56},{9,... | collective-permute-start | bytes 331784 | tf_op jit(solution)/shard_map/ppermute | solution.py:31
  132.7 2.8 %collective-permute-start.19 = (bf16[2,256,384]{2,1,0:T(8,128)(2,1)S(1)}, bf16[2,256,384]{2,1,0:T(8,128)(2,1)S(1)}, u32[]{:S(2)}, u32[]{:S(2)}) collective-permute-start(bf16[2,256,384]{2,1,0:T(8,128)(2,1)S(1)} %pad_maximum_fusion.8), channel_id=1, source_target_pairs={{0,0},{1,1},{2,2},{3,3},{4,4},{5,5},{6,6},{7,7},{8,8},{9,9},{10,10... | collective-permute-start | bytes 1179656 | tf_op jit(solution)/shard_map/ppermute | solution.py:31
  135.7 5.9 %collective-permute-done.26 = bf16[48,1152]{1,0:T(8,128)(2,1)S(1)} collective-permute-done((bf16[48,1152]{1,0:T(8,128)(2,1)S(1)}, bf16[48,1152]{1,0:T(8,128)(2,1)S(1)}, u32[]{:S(2)}, u32[]{:S(2)}) %collective-permute-start.26) | collective-permute-done | bytes 110624 | tf_op jit(solution)/shard_map/ppermute | solution.py:31
  141.8 3.4 %collective-permute-start.28 = (bf16[24,1152]{1,0:T(8,128)(2,1)S(1)}, bf16[24,1152]{1,0:T(8,128)(2,1)S(1)}, u32[]{:S(2)}, u32[]{:S(2)}) collective-permute-start(bf16[24,1152]{1,0:T(8,128)(2,1)S(1)} %get-tuple-element.71), channel_id=1, source_target_pairs={{0,8},{1,9},{2,10},{3,11},{4,12},{5,13},{6,14},{7,15},{8,0},{9,1},... | collective-permute-start | bytes 165896 | tf_op jit(solution)/shard_map/ppermute | solution.py:31
  145.2 0.4 collective-permute-start.29
  145.6 2.2 %collective-permute-done.19 = bf16[2,256,384]{2,1,0:T(8,128)(2,1)S(1)} collective-permute-done((bf16[2,256,384]{2,1,0:T(8,128)(2,1)S(1)}, bf16[2,256,384]{2,1,0:T(8,128)(2,1)S(1)}, u32[]{:S(2)}, u32[]{:S(2)}) %collective-permute-start.19) | collective-permute-done | bytes 393248 | tf_op jit(solution)/shard_map/ppermute | solution.py:31
  147.8 0.7 fusion.6
  148.5 0.7 slice_bitcast_fusion.3
  149.2 0.8 collective-permute-done.28
  150.0 0.7 pad_maximum_fusion.9
  (79 shorter events, 1.9 us)
Async XLA Ops:
  0.6 13.7 %copy-start = (s32[128,9]{0,1:T(8,128)S(1)}, s32[128,9]{0,1:T(8,128)}, u32[]{:S(2)}) copy-start(s32[128,9]{0,1:T(8,128)} %param.7) | copy-start | bytes 13828
  0.6 14.4 %collective-permute-start = (bf16[256,384]{1,0:T(8,128)(2,1)}, bf16[256,384]{1,0:T(8,128)(2,1)S(1)}, u32[]{:S(2)}, u32[]{:S(2)}) collective-permute-start(bf16[256,384]{1,0:T(8,128)(2,1)} %param.4), channel_id=1, source_target_pairs={{0,0},{1,1},{2,2},{3,3},{4,4},{5,5},{6,6},{7,7},{8,8},{9,9},{10,10... | collective-permute-start | bytes 589832 | tf_op jit(solution)/shard_map/ppermute | solution.py:31
  7.2 11.6 %collective-permute-start.1 = (bf16[256,384]{1,0:T(8,128)(2,1)}, bf16[256,384]{1,0:T(8,128)(2,1)S(1)}, u32[]{:S(2)}, u32[]{:S(2)}) collective-permute-start(bf16[256,384]{1,0:T(8,128)(2,1)} %param.4), channel_id=1, source_target_pairs={{0,2},{1,3},{2,0},{3,1},{4,6},{5,7},{6,4},{7,5},{8,10},{9,11},{10,... | collective-permute-start | bytes 589832 | tf_op jit(solution)/shard_map/ppermute | solution.py:31
  10.4 40.4 %collective-permute-start.3 = (bf16[256,384]{1,0:T(8,128)(2,1)}, bf16[256,384]{1,0:T(8,128)(2,1)S(1)}, u32[]{:S(2)}, u32[]{:S(2)}) collective-permute-start(bf16[256,384]{1,0:T(8,128)(2,1)} %param.6), channel_id=1, source_target_pairs={{0,0},{1,1},{2,2},{3,3},{4,4},{5,5},{6,6},{7,7},{8,8},{9,9},{10,10... | collective-permute-start | bytes 589832 | tf_op jit(solution)/shard_map/ppermute | solution.py:31
  18.9 12.8 %collective-permute-start.8 = (bf16[256,768]{1,0:T(8,128)(2,1)S(1)}, bf16[256,768]{1,0:T(8,128)(2,1)S(1)}, u32[]{:S(2)}, u32[]{:S(2)}) collective-permute-start(bf16[256,768]{1,0:T(8,128)(2,1)S(1)} %pad_maximum_fusion.7), channel_id=1, source_target_pairs={{0,240},{1,241},{2,242},{3,243},{4,0},{5,1},{6,2},{7,3},{8,4},{9,5... | collective-permute-start | bytes 1179656 | tf_op jit(solution)/shard_map/ppermute | solution.py:31
  22.6 9.2 %collective-permute-start.2 = (bf16[256,768]{1,0:T(8,128)(2,1)S(1)}, bf16[256,768]{1,0:T(8,128)(2,1)S(1)}, u32[]{:S(2)}, u32[]{:S(2)}) collective-permute-start(bf16[256,768]{1,0:T(8,128)(2,1)S(1)} %pad_maximum_fusion.7), channel_id=1, source_target_pairs={{0,1},{1,0},{2,3},{3,2},{4,5},{5,4},{6,7},{7,6},{8,9},{9,8},{10,11... | collective-permute-start | bytes 1179656 | tf_op jit(solution)/shard_map/ppermute | solution.py:31
  24.5 11.6 %collective-permute-start.4 = (bf16[256,768]{1,0:T(8,128)(2,1)S(1)}, bf16[256,768]{1,0:T(8,128)(2,1)S(1)}, u32[]{:S(2)}, u32[]{:S(2)}) collective-permute-start(bf16[256,768]{1,0:T(8,128)(2,1)S(1)} %pad_maximum_fusion.7), channel_id=1, source_target_pairs={{0,4},{1,5},{2,6},{3,7},{4,8},{5,9},{6,10},{7,11},{8,12},{9,13},{1... | collective-permute-start | bytes 1179656 | tf_op jit(solution)/shard_map/ppermute | solution.py:31
  31.7 11.8 %collective-permute-start.10 = (bf16[256,768]{1,0:T(8,128)(2,1)S(1)}, bf16[256,768]{1,0:T(8,128)(2,1)S(1)}, u32[]{:S(2)}, u32[]{:S(2)}) collective-permute-start(bf16[256,768]{1,0:T(8,128)(2,1)S(1)} %collective-permute-done.8), channel_id=1, source_target_pairs={{0,240},{1,241},{2,242},{3,243},{4,0},{5,1},{6,2},{7,3},{8,4},{9,5... | collective-permute-start | bytes 1179656 | tf_op jit(solution)/shard_map/ppermute | solution.py:31
  31.8 11.7 %collective-permute-start.9 = (bf16[256,768]{1,0:T(8,128)(2,1)S(1)}, bf16[256,768]{1,0:T(8,128)(2,1)S(1)}, u32[]{:S(2)}, u32[]{:S(2)}) collective-permute-start(bf16[256,768]{1,0:T(8,128)(2,1)S(1)} %collective-permute-done.8), channel_id=1, source_target_pairs={{0,1},{1,0},{2,3},{3,2},{4,5},{5,4},{6,7},{7,6},{8,9},{9,8},{10,11... | collective-permute-start | bytes 1179656 | tf_op jit(solution)/shard_map/ppermute | solution.py:31
  36.1 7.7 %collective-permute-start.7 = (bf16[256,768]{1,0:T(8,128)(2,1)S(1)}, bf16[256,768]{1,0:T(8,128)(2,1)S(1)}, u32[]{:S(2)}, u32[]{:S(2)}) collective-permute-start(bf16[256,768]{1,0:T(8,128)(2,1)S(1)} %collective-permute-done.4), channel_id=1, source_target_pairs={{0,1},{1,0},{2,3},{3,2},{4,5},{5,4},{6,7},{7,6},{8,9},{9,8},{10,11... | collective-permute-start | bytes 1179656 | tf_op jit(solution)/shard_map/ppermute | solution.py:31
  36.1 11.6 %collective-permute-start.5 = (bf16[256,768]{1,0:T(8,128)(2,1)S(1)}, bf16[256,768]{1,0:T(8,128)(2,1)S(1)}, u32[]{:S(2)}, u32[]{:S(2)}) collective-permute-start(bf16[256,768]{1,0:T(8,128)(2,1)S(1)} %collective-permute-done.4), channel_id=1, source_target_pairs={{0,4},{1,5},{2,6},{3,7},{4,8},{5,9},{6,10},{7,11},{8,12},{9,13},{1... | collective-permute-start | bytes 1179656 | tf_op jit(solution)/shard_map/ppermute | solution.py:31
  43.5 5.1 %collective-permute-start.11 = (bf16[256,768]{1,0:T(8,128)(2,1)S(1)}, bf16[256,768]{1,0:T(8,128)(2,1)S(1)}, u32[]{:S(2)}, u32[]{:S(2)}) collective-permute-start(bf16[256,768]{1,0:T(8,128)(2,1)S(1)} %collective-permute-done.10), channel_id=1, source_target_pairs={{0,1},{1,0},{2,3},{3,2},{4,5},{5,4},{6,7},{7,6},{8,9},{9,8},{10,11... | collective-permute-start | bytes 1179656 | tf_op jit(solution)/shard_map/ppermute | solution.py:31
  47.7 2.0 %collective-permute-start.6 = (bf16[256,768]{1,0:T(8,128)(2,1)S(1)}, bf16[256,768]{1,0:T(8,128)(2,1)S(1)}, u32[]{:S(2)}, u32[]{:S(2)}) collective-permute-start(bf16[256,768]{1,0:T(8,128)(2,1)S(1)} %collective-permute-done.5), channel_id=1, source_target_pairs={{0,1},{1,0},{2,3},{3,2},{4,5},{5,4},{6,7},{7,6},{8,9},{9,8},{10,11... | collective-permute-start | bytes 1179656 | tf_op jit(solution)/shard_map/ppermute | solution.py:31
  57.0 0.9 copy-start.7
  57.9 0.7 copy-start.11
  58.6 10.7 %copy-start.9 = (bf16[256,384]{1,0:T(8,128)(2,1)}, bf16[256,384]{1,0:T(8,128)(2,1)S(1)}, u32[]{:S(2)}) copy-start(bf16[256,384]{1,0:T(8,128)(2,1)S(1)} %get-tuple-element.31.dq_ref) | copy-start | bytes 589828
  58.6 14.0 %collective-permute-start.16 = (bf16[256,768]{1,0:T(8,128)(2,1)S(1)}, bf16[256,768]{1,0:T(8,128)(2,1)S(1)}, u32[]{:S(2)}, u32[]{:S(2)}) collective-permute-start(bf16[256,768]{1,0:T(8,128)(2,1)S(1)} %get-tuple-element.37.refs_9_), channel_id=1, source_target_pairs={{0,4},{1,5},{2,6},{3,7},{4,8},{5,9},{6,10},{7,11},{8,12},{9,13},{1... | collective-permute-start | bytes 1179656 | tf_op jit(solution)/shard_map/ppermute | solution.py:31
  63.2 17.6 %collective-permute-start.14 = (bf16[256,768]{1,0:T(8,128)(2,1)S(1)}, bf16[256,768]{1,0:T(8,128)(2,1)S(1)}, u32[]{:S(2)}, u32[]{:S(2)}) collective-permute-start(bf16[256,768]{1,0:T(8,128)(2,1)S(1)} %get-tuple-element.33.refs_5_), channel_id=1, source_target_pairs={{0,240},{1,241},{2,242},{3,243},{4,0},{5,1},{6,2},{7,3},{8,4},{9,5... | collective-permute-start | bytes 1179656 | tf_op jit(solution)/shard_map/ppermute | solution.py:31
  69.3 23.3 %copy-start.1 = (bf16[2,4,48,1152]{3,2,1,0:T(8,128)(2,1)S(1)}, bf16[2,4,48,1152]{3,2,1,0:T(8,128)(2,1)}, u32[]{:S(2)}) copy-start(bf16[2,4,48,1152]{3,2,1,0:T(8,128)(2,1)} %get-tuple-element.38.refs_0_) | copy-start | bytes 2654212
  69.3 23.3 %copy-start.2 = (bf16[2,4,48,1152]{3,2,1,0:T(8,128)(2,1)S(1)}, bf16[2,4,48,1152]{3,2,1,0:T(8,128)(2,1)}, u32[]{:S(2)}) copy-start(bf16[2,4,48,1152]{3,2,1,0:T(8,128)(2,1)} %get-tuple-element.39.refs_1_) | copy-start | bytes 2654212
  69.3 22.4 %collective-permute-start.12 = (bf16[2,4,48,1152]{3,2,1,0:T(8,128)(2,1)}, bf16[2,4,48,1152]{3,2,1,0:T(8,128)(2,1)S(1)}, u32[]{:S(2)}, u32[]{:S(2)}) collective-permute-start(bf16[2,4,48,1152]{3,2,1,0:T(8,128)(2,1)} %get-tuple-element.40), channel_id=1, source_target_pairs={{0,64},{1,65},{2,66},{3,67},{4,68},{5,69},{6,70},{7,71},{8,72},{9,... | collective-permute-start | bytes 2654216 | tf_op jit(solution)/shard_map/ppermute | solution.py:31
  70.8 21.7 %collective-permute-start.13 = (bf16[2,4,48,1152]{3,2,1,0:T(8,128)(2,1)}, bf16[2,4,48,1152]{3,2,1,0:T(8,128)(2,1)S(1)}, u32[]{:S(2)}, u32[]{:S(2)}) collective-permute-start(bf16[2,4,48,1152]{3,2,1,0:T(8,128)(2,1)} %get-tuple-element.41), channel_id=1, source_target_pairs={{0,16},{1,17},{2,18},{3,19},{4,20},{5,21},{6,22},{7,23},{8,24},{9,... | collective-permute-start | bytes 2654216 | tf_op jit(solution)/shard_map/ppermute | solution.py:31
  73.4 30.0 %collective-permute-start.17 = (bf16[256,768]{1,0:T(8,128)(2,1)}, bf16[256,768]{1,0:T(8,128)(2,1)}, u32[]{:S(2)}, u32[]{:S(2)}) collective-permute-start(bf16[256,768]{1,0:T(8,128)(2,1)} %add_convert_fusion.1), channel_id=1, source_target_pairs={{0,4},{1,5},{2,6},{3,7},{4,8},{5,9},{6,10},{7,11},{8,12},{9,13},{1... | collective-permute-start | bytes 1179656 | tf_op jit(solution)/shard_map/ppermute | solution.py:31
  81.6 26.6 %collective-permute-start.15 = (bf16[256,768]{1,0:T(8,128)(2,1)}, bf16[256,768]{1,0:T(8,128)(2,1)}, u32[]{:S(2)}, u32[]{:S(2)}) collective-permute-start(bf16[256,768]{1,0:T(8,128)(2,1)} %add_convert_fusion.2), channel_id=1, source_target_pairs={{0,240},{1,241},{2,242},{3,243},{4,0},{5,1},{6,2},{7,3},{8,4},{9,5... | collective-permute-start | bytes 1179656 | tf_op jit(solution)/shard_map/ppermute | solution.py:31
  92.6 15.6 %copy-start.8 = (f32[256,768]{1,0:T(8,128)S(1)}, f32[256,768]{1,0:T(8,128)}, u32[]{:S(2)}) copy-start(f32[256,768]{1,0:T(8,128)} %copy-done.7) | copy-start | bytes 2359300
  92.6 15.6 %copy-start.10 = (bf16[256,384]{1,0:T(8,128)(2,1)S(1)}, bf16[256,384]{1,0:T(8,128)(2,1)}, u32[]{:S(2)}) copy-start(bf16[256,384]{1,0:T(8,128)(2,1)} %copy-done.9) | copy-start | bytes 589828
  93.8 0.9 copy-start.5
  94.7 17.5 %copy-start.3 = (f32[4,48,1152]{2,1,0:T(8,128)}, f32[4,48,1152]{2,1,0:T(8,128)S(1)}, u32[]{:S(2)}) copy-start(f32[4,48,1152]{2,1,0:T(8,128)S(1)} %get-tuple-element.47.refs_0_) | copy-start | bytes 2654212
  94.7 17.7 %collective-permute-start.20 = (bf16[4,48,1152]{2,1,0:T(8,128)(2,1)}, bf16[4,48,1152]{2,1,0:T(8,128)(2,1)S(1)}, u32[]{:S(2)}, u32[]{:S(2)}) collective-permute-start(bf16[4,48,1152]{2,1,0:T(8,128)(2,1)} %get-tuple-element.42), channel_id=1, source_target_pairs={{0,192},{1,193},{2,194},{3,195},{4,196},{5,197},{6,198},{7,199},{8... | collective-permute-start | bytes 1327112 | tf_op jit(solution)/shard_map/ppermute | solution.py:31
  100.6 16.8 %collective-permute-start.21 = (bf16[4,48,1152]{2,1,0:T(8,128)(2,1)}, bf16[4,48,1152]{2,1,0:T(8,128)(2,1)S(1)}, u32[]{:S(2)}, u32[]{:S(2)}) collective-permute-start(bf16[4,48,1152]{2,1,0:T(8,128)(2,1)} %get-tuple-element.49), channel_id=1, source_target_pairs={{0,48},{1,49},{2,50},{3,51},{4,52},{5,53},{6,54},{7,55},{8,56},{9,... | collective-permute-start | bytes 1327112 | tf_op jit(solution)/shard_map/ppermute | solution.py:31
  108.2 9.3 %copy-start.6 = (f32[4,48,1152]{2,1,0:T(8,128)S(1)}, f32[4,48,1152]{2,1,0:T(8,128)}, u32[]{:S(2)}) copy-start(f32[4,48,1152]{2,1,0:T(8,128)} %copy-done.5) | copy-start | bytes 2654212
  112.3 7.2 %collective-permute-start.18 = (bf16[2,256,384]{2,1,0:T(8,128)(2,1)S(1)}, bf16[2,256,384]{2,1,0:T(8,128)(2,1)}, u32[]{:S(2)}, u32[]{:S(2)}) collective-permute-start(bf16[2,256,384]{2,1,0:T(8,128)(2,1)S(1)} %get-tuple-element.46), channel_id=1, source_target_pairs={{0,1},{1,0},{2,3},{3,2},{4,5},{5,4},{6,7},{7,6},{8,9},{9,8},{10,11... | collective-permute-start | bytes 1179656 | tf_op jit(solution)/shard_map/ppermute | solution.py:31
  117.5 1.2 copy-start.4
  119.4 7.4 %collective-permute-start.23 = (bf16[2,48,1152]{2,1,0:T(8,128)(2,1)S(1)}, bf16[2,48,1152]{2,1,0:T(8,128)(2,1)S(1)}, u32[]{:S(2)}, u32[]{:S(2)}) collective-permute-start(bf16[2,48,1152]{2,1,0:T(8,128)(2,1)S(1)} %get-tuple-element.53), channel_id=1, source_target_pairs={{0,64},{1,65},{2,66},{3,67},{4,68},{5,69},{6,70},{7,71},{8,72},{9,... | collective-permute-start | bytes 663560 | tf_op jit(solution)/shard_map/ppermute | solution.py:31
  119.5 13.2 %copy-start.12 = (bf16[256,384]{1,0:T(8,128)(2,1)S(1)}, bf16[256,384]{1,0:T(8,128)(2,1)}, u32[]{:S(2)}) copy-start(bf16[256,384]{1,0:T(8,128)(2,1)} %copy-done.11) | copy-start | bytes 589828
  120.7 8.1 %collective-permute-start.24 = (bf16[256,384]{1,0:T(8,128)(2,1)S(1)}, bf16[256,384]{1,0:T(8,128)(2,1)S(1)}, u32[]{:S(2)}, u32[]{:S(2)}) collective-permute-start(bf16[256,384]{1,0:T(8,128)(2,1)S(1)} %get-tuple-element.72), channel_id=1, source_target_pairs={{0,2},{1,3},{2,0},{3,1},{4,6},{5,7},{6,4},{7,5},{8,10},{9,11},{10,... | collective-permute-start | bytes 589832 | tf_op jit(solution)/shard_map/ppermute | solution.py:31
  120.8 7.4 %collective-permute-start.22 = (bf16[2,48,1152]{2,1,0:T(8,128)(2,1)S(1)}, bf16[2,48,1152]{2,1,0:T(8,128)(2,1)S(1)}, u32[]{:S(2)}, u32[]{:S(2)}) collective-permute-start(bf16[2,48,1152]{2,1,0:T(8,128)(2,1)S(1)} %get-tuple-element.51), channel_id=1, source_target_pairs={{0,16},{1,17},{2,18},{3,19},{4,20},{5,21},{6,22},{7,23},{8,24},{9,... | collective-permute-start | bytes 663560 | tf_op jit(solution)/shard_map/ppermute | solution.py:31
  128.8 6.9 %collective-permute-start.25 = (bf16[48,1152]{1,0:T(8,128)(2,1)S(1)}, bf16[48,1152]{1,0:T(8,128)(2,1)S(1)}, u32[]{:S(2)}, u32[]{:S(2)}) collective-permute-start(bf16[48,1152]{1,0:T(8,128)(2,1)S(1)} %fusion.7), channel_id=1, source_target_pairs={{0,48},{1,49},{2,50},{3,51},{4,52},{5,53},{6,54},{7,55},{8,56},{9,... | collective-permute-start | bytes 331784 | tf_op jit(solution)/shard_map/ppermute | solution.py:31
  132.7 15.1 %collective-permute-start.19 = (bf16[2,256,384]{2,1,0:T(8,128)(2,1)S(1)}, bf16[2,256,384]{2,1,0:T(8,128)(2,1)S(1)}, u32[]{:S(2)}, u32[]{:S(2)}) collective-permute-start(bf16[2,256,384]{2,1,0:T(8,128)(2,1)S(1)} %pad_maximum_fusion.8), channel_id=1, source_target_pairs={{0,0},{1,1},{2,2},{3,3},{4,4},{5,5},{6,6},{7,7},{8,8},{9,9},{10,10... | collective-permute-start | bytes 1179656 | tf_op jit(solution)/shard_map/ppermute | solution.py:31
  135.6 6.0 %collective-permute-start.26 = (bf16[48,1152]{1,0:T(8,128)(2,1)S(1)}, bf16[48,1152]{1,0:T(8,128)(2,1)S(1)}, u32[]{:S(2)}, u32[]{:S(2)}) collective-permute-start(bf16[48,1152]{1,0:T(8,128)(2,1)S(1)} %fusion.8), channel_id=1, source_target_pairs={{0,192},{1,193},{2,194},{3,195},{4,196},{5,197},{6,198},{7,199},{8... | collective-permute-start | bytes 331784 | tf_op jit(solution)/shard_map/ppermute | solution.py:31
  141.7 7.5 %collective-permute-start.27 = (bf16[24,1152]{1,0:T(8,128)(2,1)S(1)}, bf16[24,1152]{1,0:T(8,128)(2,1)S(1)}, u32[]{:S(2)}, u32[]{:S(2)}) collective-permute-start(bf16[24,1152]{1,0:T(8,128)(2,1)S(1)} %get-tuple-element.69), channel_id=1, source_target_pairs={{0,4},{1,5},{2,6},{3,7},{4,8},{5,9},{6,10},{7,11},{8,12},{9,13},{1... | collective-permute-start | bytes 165896 | tf_op jit(solution)/shard_map/ppermute | solution.py:31
  141.8 8.2 %collective-permute-start.28 = (bf16[24,1152]{1,0:T(8,128)(2,1)S(1)}, bf16[24,1152]{1,0:T(8,128)(2,1)S(1)}, u32[]{:S(2)}, u32[]{:S(2)}) collective-permute-start(bf16[24,1152]{1,0:T(8,128)(2,1)S(1)} %get-tuple-element.71), channel_id=1, source_target_pairs={{0,8},{1,9},{2,10},{3,11},{4,12},{5,13},{6,14},{7,15},{8,0},{9,1},... | collective-permute-start | bytes 165896 | tf_op jit(solution)/shard_map/ppermute | solution.py:31
  145.2 4.7 %collective-permute-start.29 = (bf16[24,1152]{1,0:T(8,128)(2,1)S(1)}, bf16[24,1152]{1,0:T(8,128)(2,1)S(1)}, u32[]{:S(2)}, u32[]{:S(2)}) collective-permute-start(bf16[24,1152]{1,0:T(8,128)(2,1)S(1)} %get-tuple-element.70), channel_id=1, source_target_pairs={{0,12},{1,13},{2,14},{3,15},{4,0},{5,1},{6,2},{7,3},{8,4},{9,5},{1... | collective-permute-start | bytes 165896 | tf_op jit(solution)/shard_map/ppermute | solution.py:31
where the time goes:
time: 151 us
  waiting for transfers between devices  58.2 us (39%)
  starting transfers between devices  54.2 us (36%)
  Pallas kernels  18.3 us (12%)
  local copies, waits for them, and re-layouts  7.16 us (5%)
  matrix products  5.83 us (4%)
  other arithmetic  5.7 us (4%)
    ppermute x30, waiting for transfers between devices, move(): lax.ppermute(value, AXES, [(i, flat(*to(*coords(i)))) for i in range(256)])  58.2 us
    ppermute x30, starting transfers between devices, move(): lax.ppermute(value, AXES, [(i, flat(*to(*coords(i)))) for i in range(256)])  54.2 us
    pallas_call x1, Pallas kernels, attention(): pl.pallas_call(attention_kernel, out_shape=[jax.ShapeDtypeStruct((rows, w...  6.21 us
    pallas_call x1, Pallas kernels, weight_terms(): pl.pallas_call(weight_kernel, out_shape=[jax.ShapeDtypeStruct(shape, BF16...  6.09 us
    dot_general x6, matrix products, dot(): return lax.dot_general(a, b, dims, preferred_element_type=F32)  5.83 us
    pallas_call x1, Pallas kernels, input_terms(): pl.pallas_call(input_kernel, out_shape=[jax.ShapeDtypeStruct((2, rows, wi...  4.03 us
    unnamed x28, local copies, waits for them, and re-layouts  3.7 us
  transfers between devices with their start and end apart: 30, of which 16 were waited for; matrix products, arithmetic and copies ran while one was open for 9% of the time, Pallas kernels for 8%

commit v1 on v0

--- a/solution.py
+++ b/solution.py
@@ -277,17 +277,21 @@
     return 3 - i
 
 
+def firstly(i, c):
+    return jnp.where(c == 0, flip(i), wrap(i)) if isinstance(c, jax.Array) else (wrap if c else flip)(i)
+
+
+def secondly(i, c):
+    return firstly(i, 1 - c)
+
+
 def partner(axis, rule):
     def to(*at):
-        at = list(at)
-        at[axis] = rule(at[axis])
-        return tuple(at)
+        to_at = list(at)
+        to_at[axis] = rule(at[axis], at[4])
+        return tuple(to_at)
 
     return to
-
-
-def onward(axis, step):
-    return partner(axis, lambda i: (i + step) % SIDE)
 
 
 def swapped(value):
@@ -303,8 +307,9 @@
     weight_q = proj_weight[0]
     weight_kv = jnp.concatenate([proj_weight[1], proj_weight[2]], axis=-1)
 
+    far = move(activations, lambda x, y, z, h, c: (x, y, turned(y, z), 1 - h, c))
     near = reversal(activations)
-    far = move(activations, lambda x, y, z, h, c: (x, y, turned(y, z), 1 - h, c))
+    far, weight_kv = lax.optimization_barrier((far, weight_kv))
     pair = jnp.concatenate([jnp.where(h == 0, near, far), jnp.where(h == 0, far, near)], axis=1)
 
     def full(mine, theirs):
@@ -336,15 +341,18 @@
         halo.append(along_chain(passed.astype(BF16), way))
 
     order = jnp.stack(
-        [jnp.stack([flip(i), wrap(flip(i)), i, wrap(i)]) for i in (x, y)]
+        [
+            jnp.stack([firstly(i, c), secondly(firstly(i, c), c), i, secondly(i, c)])
+            for i in (x, y)
+        ]
     ).astype(jnp.int32)
     sent_x, kept_x, sent_y, kept_y = weight_terms(order, grad_query, tokens, grads)
-    got = [move(sent_x, partner(0, flip)), move(sent_y, partner(1, flip))]
+    got = [move(sent_x, partner(0, firstly)), move(sent_y, partner(1, firstly))]
     pass_x, pass_y, *sums = first_sums((kept_x, kept_y), got)
     pass_one = pass_x
-    got = [move(pass_x, partner(0, wrap)), move(pass_y, partner(1, wrap))]
+    got = [move(pass_x, partner(0, secondly)), move(pass_y, partner(1, secondly))]
     sent_x, sent_y, kept_x, kept_y = second_sums(order, sums, got)
-    got_x, got_y = move(sent_x, partner(1, flip)), move(sent_y, partner(0, flip))
+    got_x, got_y = move(sent_x, partner(1, firstly)), move(sent_y, partner(0, firstly))
     place = jnp.stack([1 - c, 3 - c, c, 2 + c]).astype(jnp.int32)
     halo = lax.optimization_barrier((pass_one, *halo))[1:]
     sent, kept = input_terms(place, grad_query, own, proj_weight, halo)
@@ -356,8 +364,8 @@
     pass_x = (kept_x[1] + got_x[1].astype(F32)).astype(BF16)
     pass_y = (kept_y[1] + got_y[1].astype(F32)).astype(BF16)
     pass_x, pass_y, home_far = lax.optimization_barrier((pass_x, pass_y, home_far))
-    keep_x = kept_x[0] + got_x[0].astype(F32) + move(pass_x, partner(1, wrap)).astype(F32)
-    keep_y = kept_y[0] + got_y[0].astype(F32) + move(pass_y, partner(0, wrap)).astype(F32)
+    keep_x = kept_x[0] + got_x[0].astype(F32) + move(pass_x, partner(1, secondly)).astype(F32)
+    keep_y = kept_y[0] + got_y[0].astype(F32) + move(pass_y, partner(0, secondly)).astype(F32)
 
     chunks = jnp.concatenate([keep_x, keep_y], axis=0).reshape(SIDE, 24, 3 * width)
     mine = exchanged(chunks, 2, z)

time: 151 us -> 140 us (0.927)
  waiting for transfers between devices: 58.2 us -> 46.3 us
  other arithmetic: 5.7 us -> 7.96 us
    ppermute x30, waiting for transfers between devices: 58.2 us -> 46.3 us  [move(): lax.ppermute(value, AXES, [(i, flat(*to(*coords(i)))) for i in range(256)])]
    concatenate x0 -> x1, other arithmetic: none -> 1.59 us  [local(): weight_kv = jnp.concatenate([proj_weight[1], proj_weight[2]], axis=-1)]
    unnamed x28 -> x30, local copies, waits for them, and re-layouts: 3.7 us -> 3.69 us
  transfers between devices with their start and end apart: 30 -> 30, of which waited for: 16 -> 16; matrix products, arithmetic and copies ran while one was open for 9% -> 12% of each run, Pallas kernels for 8% -> 9%
where the time goes in v1:
time: 140 us
  starting transfers between devices  53 us (38%)
  waiting for transfers between devices  46.3 us (33%)
  Pallas kernels  18.3 us (13%)
  other arithmetic  7.96 us (6%)
  local copies, waits for them, and re-layouts  7.16 us (5%)
  matrix products  5.96 us (4%)
    ppermute x30, starting transfers between devices, move(): lax.ppermute(value, AXES, [(i, flat(*to(*coords(i)))) for i in range(256)])  53 us
    ppermute x30, waiting for transfers between devices, move(): lax.ppermute(value, AXES, [(i, flat(*to(*coords(i)))) for i in range(256)])  46.3 us
    pallas_call x1, Pallas kernels, attention(): pl.pallas_call(attention_kernel, out_shape=[jax.ShapeDtypeStruct((rows, w...  6.21 us
    pallas_call x1, Pallas kernels, weight_terms(): pl.pallas_call(weight_kernel, out_shape=[jax.ShapeDtypeStruct(shape, BF16...  6.09 us
    dot_general x6, matrix products, dot(): return lax.dot_general(a, b, dims, preferred_element_type=F32)  5.96 us
    pallas_call x1, Pallas kernels, input_terms(): pl.pallas_call(input_kernel, out_shape=[jax.ShapeDtypeStruct((2, rows, wi...  4.03 us
    unnamed x30, local copies, waits for them, and re-layouts  3.69 us
  transfers between devices with their start and end apart: 30, of which 16 were waited for; matrix products, arithmetic and copies ran while one was open for 12% of the time, Pallas kernels for 9%

profile of v1, /device:TPU:24, one launch (start us, length us, event | category | flops | bytes accessed | tf_op | source)
XLA Modules:
  0.0 139.9 jit_solution(11056592687558947024)
XLA Ops:
  0.6 6.5 %collective-permute-start = (bf16[256,384]{1,0:T(8,128)(2,1)}, bf16[256,384]{1,0:T(8,128)(2,1)S(1)}, u32[]{:S(2)}, u32[]{:S(2)}) collective-permute-start(bf16[256,384]{1,0:T(8,128)(2,1)} %param.4), channel_id=1, source_target_pairs={{0,0},{1,1},{2,2},{3,3},{4,4},{5,5},{6,6},{7,7},{8,8},{9,9},{10,10... | collective-permute-start | bytes 589832 | tf_op jit(solution)/shard_map/ppermute | solution.py:31
  7.2 3.2 %collective-permute-start.1 = (bf16[256,384]{1,0:T(8,128)(2,1)}, bf16[256,384]{1,0:T(8,128)(2,1)S(1)}, u32[]{:S(2)}, u32[]{:S(2)}) collective-permute-start(bf16[256,384]{1,0:T(8,128)(2,1)} %param.4), channel_id=1, source_target_pairs={{0,2},{1,3},{2,0},{3,1},{4,6},{5,7},{6,4},{7,5},{8,10},{9,11},{10,... | collective-permute-start | bytes 589832 | tf_op jit(solution)/shard_map/ppermute | solution.py:31
  10.4 3.8 %collective-permute-start.3 = (bf16[256,384]{1,0:T(8,128)(2,1)}, bf16[256,384]{1,0:T(8,128)(2,1)S(1)}, u32[]{:S(2)}, u32[]{:S(2)}) collective-permute-start(bf16[256,384]{1,0:T(8,128)(2,1)} %param.6), channel_id=1, source_target_pairs={{0,0},{1,1},{2,2},{3,3},{4,4},{5,5},{6,6},{7,7},{8,8},{9,9},{10,10... | collective-permute-start | bytes 589832 | tf_op jit(solution)/shard_map/ppermute | solution.py:31
  14.3 1.9 %slice_bitcast_fusion.1 = (bf16[1536,384]{1,0:T(8,128)(2,1)S(1)}, bf16[1536,384]{1,0:T(8,128)(2,1)S(1)}) fusion(bf16[3,1536,384]{2,1,0:T(8,128)(2,1)} %weight_ref.1), kind=kLoop, calls=%fused_computation.10 | loop fusion | bytes 4718592 | tf_op jit(solution)/shard_map/squeeze | solution.py:308
  16.3 0.1 copy.8
  16.4 1.6 %pad_maximum_fusion = bf16[1536,768]{1,0:T(8,128)(2,1)} fusion(bf16[1536,384]{1,0:T(8,128)(2,1)S(1)} %get-tuple-element.62, bf16[1536,384]{1,0:T(8,128)(2,1)S(1)} %get-tuple-element.61), kind=kLoop, calls=%fused_computation | loop fusion | flops 4718592 | bytes 4718592 | tf_op jit(solution)/shard_map/concatenate | solution.py:308
  18.0 0.2 compare_reduce_fusion
  18.2 0.6 collective-permute-done.1
  18.9 0.8 pad_maximum_fusion.7
  19.7 0.1 copy.9
  20.0 3.7 %collective-permute-start.8 = (bf16[256,768]{1,0:T(8,128)(2,1)}, bf16[256,768]{1,0:T(8,128)(2,1)S(1)}, u32[]{:S(2)}, u32[]{:S(2)}) collective-permute-start(bf16[256,768]{1,0:T(8,128)(2,1)} %pad_maximum_fusion.7), channel_id=1, source_target_pairs={{0,240},{1,241},{2,242},{3,243},{4,0},{5,1},{6,2},{7,3},{8,4},{9,5... | collective-permute-start | bytes 1179656 | tf_op jit(solution)/shard_map/ppermute | solution.py:31
  23.8 0.1 broadcast_select_fusion.9
  24.0 9.7 %collective-permute-done.4 = bf16[256,768]{1,0:T(8,128)(2,1)S(1)} collective-permute-done((bf16[256,768]{1,0:T(8,128)(2,1)}, bf16[256,768]{1,0:T(8,128)(2,1)S(1)}, u32[]{:S(2)}, u32[]{:S(2)}) %collective-permute-start.4) | collective-permute-done | bytes 393248 | tf_op jit(solution)/shard_map/ppermute | solution.py:31
  33.7 2.0 %fusion.3.q_ref = bf16[256,384]{1,0:T(8,128)(2,1)S(1)} fusion(bf16[3,1536,384]{2,1,0:T(8,128)(2,1)} %weight_ref.1, bf16[256,384]{1,0:T(8,128)(2,1)S(1)} %get-tuple-element.105, bf16[256,384]{1,0:T(8,128)(2,1)S(1)} %get-tuple-element.95, bf16[256,384]{1,0:T(8,128)(2,1)S(1)} %get-tuple-element.106, bf16[256,384]{1,0:T(8,128)(2,1)S(1)} %get-tuple-element.94), kind=kOutput, calls=%fused_computation.11 | convolution fusion | flops 305233920 | bytes 2162688 | tf_op jit(solution)/shard_map/dot_general | solution.py:64
  35.8 0.6 collective-permute-start.5
  36.3 0.2 collective-permute-start.9
  36.6 1.6 %collective-permute-start.10 = (bf16[256,768]{1,0:T(8,128)(2,1)S(1)}, bf16[256,768]{1,0:T(8,128)(2,1)S(1)}, u32[]{:S(2)}, u32[]{:S(2)}) collective-permute-start(bf16[256,768]{1,0:T(8,128)(2,1)S(1)} %collective-permute-done.8), channel_id=1, source_target_pairs={{0,240},{1,241},{2,242},{3,243},{4,0},{5,1},{6,2},{7,3},{8,4},{9,5... | collective-permute-start | bytes 1179656 | tf_op jit(solution)/shard_map/ppermute | solution.py:31
  38.2 0.8 convolution_convert_fusion.2.refs_2_
  39.3 0.8 convolution_convert_fusion.3.refs_1_
  40.1 7.2 %collective-permute-done.5 = bf16[256,768]{1,0:T(8,128)(2,1)S(1)} collective-permute-done((bf16[256,768]{1,0:T(8,128)(2,1)S(1)}, bf16[256,768]{1,0:T(8,128)(2,1)S(1)}, u32[]{:S(2)}, u32[]{:S(2)}) %collective-permute-start.5) | collective-permute-done | bytes 393248 | tf_op jit(solution)/shard_map/ppermute | solution.py:31
  47.5 2.5 %collective-permute-done.10 = bf16[256,768]{1,0:T(8,128)(2,1)S(1)} collective-permute-done((bf16[256,768]{1,0:T(8,128)(2,1)S(1)}, bf16[256,768]{1,0:T(8,128)(2,1)S(1)}, u32[]{:S(2)}, u32[]{:S(2)}) %collective-permute-start.10) | collective-permute-done | bytes 393248 | tf_op jit(solution)/shard_map/ppermute | solution.py:31
  50.0 0.8 convolution_convert_fusion.1.refs_3_
  50.9 0.1 fusion.21
  51.0 0.8 convolution_convert_fusion.4.refs_0_
  51.9 0.1 fusion.15
  52.0 0.8 convolution_convert_fusion.refs_4_
  52.9 6.2 %shard_map.67 = (bf16[256,384]{1,0:T(8,128)(2,1)S(1)}, bf16[256,384]{1,0:T(8,128)(2,1)S(1)}, f32[256,768]{1,0:T(8,128)S(1)}, bf16[256,768]{1,0:T(8,128)(2,1)S(1)...) custom-call(bf16[256,384]{1,0:T(8,128)(2,1)S(1)} %fusion.3.q_ref, ...), custom_call_target="tpu_custom_call" | custom-call | flops 1509949440 | bytes 3932160 | tf_op jit(solution)/shard_map/pallas_call | solution.py:115
  59.2 0.9 copy-done.7
  60.0 0.7 copy-done.11
  60.8 4.1 %collective-permute-start.16 = (bf16[256,768]{1,0:T(8,128)(2,1)S(1)}, bf16[256,768]{1,0:T(8,128)(2,1)S(1)}, u32[]{:S(2)}, u32[]{:S(2)}) collective-permute-start(bf16[256,768]{1,0:T(8,128)(2,1)S(1)} %get-tuple-element.41.refs_9_), channel_id=1, source_target_pairs={{0,4},{1,5},{2,6},{3,7},{4,8},{5,9},{6,10},{7,11},{8,12},{9,13},{1... | collective-permute-start | bytes 1179656 | tf_op jit(solution)/shard_map/ppermute | solution.py:31
  64.8 6.1 %shard_map.68 = (bf16[2,4,48,1152]{3,2,1,0:T(8,128)(2,1)}, bf16[2,4,48,1152]{3,2,1,0:T(8,128)(2,1)}, bf16[2,4,48,1152]{3,2,1,0:T(8,128)(2,1)}, bf16[2,4,48,1152]{3,2,1,0:T(8,128)(2,1)}) custom-call(s32[2,4]{1,0:T(2,128)S(1)} %pad_add_fusion.order_ref, bf16[256,384]{1,0:T(8,128)(2,1)S(1)} %get-tuple-element.35.dq_ref, ...), custom_call_target="tpu_custom_call" | custom-call | flops 3300000000 | bytes 30000000 | tf_op jit(solution)/shard_map/pallas_call | solution.py:171
  70.9 1.6 %collective-permute-start.12 = (bf16[2,4,48,1152]{3,2,1,0:T(8,128)(2,1)}, bf16[2,4,48,1152]{3,2,1,0:T(8,128)(2,1)S(1)}, u32[]{:S(2)}, u32[]{:S(2)}) collective-permute-start(bf16[2,4,48,1152]{3,2,1,0:T(8,128)(2,1)} %get-tuple-element.44), channel_id=1, source_target_pairs={{0,64},{1,193},{2,66},{3,195},{4,68},{5,197},{6,70},{7,199},{8,72}... | collective-permute-start | bytes 2654216 | tf_op jit(solution)/shard_map/ppermute | solution.py:31
  72.5 1.8 %collective-permute-done.14 = bf16[256,768]{1,0:T(8,128)(2,1)S(1)} collective-permute-done((bf16[256,768]{1,0:T(8,128)(2,1)S(1)}, bf16[256,768]{1,0:T(8,128)(2,1)S(1)}, u32[]{:S(2)}, u32[]{:S(2)}) %collective-permute-start.14) | collective-permute-done | bytes 393248 | tf_op jit(solution)/shard_map/ppermute | solution.py:31
  74.3 0.9 add_convert_fusion.2
  75.2 0.9 add_convert_fusion.1
  76.1 4.1 %collective-permute-start.17 = (bf16[256,768]{1,0:T(8,128)(2,1)}, bf16[256,768]{1,0:T(8,128)(2,1)}, u32[]{:S(2)}, u32[]{:S(2)}) collective-permute-start(bf16[256,768]{1,0:T(8,128)(2,1)} %add_convert_fusion.1), channel_id=1, source_target_pairs={{0,4},{1,5},{2,6},{3,7},{4,8},{5,9},{6,10},{7,11},{8,12},{9,13},{1... | collective-permute-start | bytes 1179656 | tf_op jit(solution)/shard_map/ppermute | solution.py:31
  80.2 4.1 %collective-permute-done.12.refs_2_ = bf16[2,4,48,1152]{3,2,1,0:T(8,128)(2,1)S(1)} collective-permute-done((bf16[2,4,48,1152]{3,2,1,0:T(8,128)(2,1)}, bf16[2,4,48,1152]{3,2,1,0:T(8,128)(2,1)S(1)}, u32[]{:S(2)}, u32[]{:S(2)}) %collective-permute-start.12) | collective-permute-done | bytes 884768 | tf_op jit(solution)/shard_map/ppermute | solution.py:31
  84.3 1.5 %collective-permute-done.13.refs_3_ = bf16[2,4,48,1152]{3,2,1,0:T(8,128)(2,1)S(1)} collective-permute-done((bf16[2,4,48,1152]{3,2,1,0:T(8,128)(2,1)}, bf16[2,4,48,1152]{3,2,1,0:T(8,128)(2,1)S(1)}, u32[]{:S(2)}, u32[]{:S(2)}) %collective-permute-start.13) | collective-permute-done | bytes 884768 | tf_op jit(solution)/shard_map/ppermute | solution.py:31
  85.8 1.2 shard_map.69
  87.0 0.9 copy-done.5
  87.9 9.1 %collective-permute-start.20 = (bf16[4,48,1152]{2,1,0:T(8,128)(2,1)}, bf16[4,48,1152]{2,1,0:T(8,128)(2,1)S(1)}, u32[]{:S(2)}, u32[]{:S(2)}) collective-permute-start(bf16[4,48,1152]{2,1,0:T(8,128)(2,1)} %get-tuple-element.46), channel_id=1, source_target_pairs={{0,192},{1,65},{2,194},{3,67},{4,196},{5,69},{6,198},{7,71},{8,200... | collective-permute-start | bytes 1327112 | tf_op jit(solution)/shard_map/ppermute | solution.py:31
  97.2 4.0 %shard_map.70 = (bf16[2,256,384]{2,1,0:T(8,128)(2,1)S(1)}, f32[2,256,384]{2,1,0:T(8,128)S(1)}) custom-call(s32[4]{0:T(128)S(1)} %pad_add_fusion.1.place_ref, bf16[256,384]{1,0:T(8,128)(2,1)S(1)} %copy-done.10, f32[256,768]{1,0:T(8,128)S(1)} %copy-done.8, bf16[3,1536,384]{2,1,0:T(8,128)(2,1)} %weight_ref.1, bf16[256,768]{1,0:T(8,128)(2,1)} %collective-permute-done.15.refs_0_, ...), custom_call_target="tpu_custom_call" | custom-call | tf_op jit(solution)/shard_map/pallas_call | solution.py:246
  101.2 4.5 %collective-permute-start.18 = (bf16[2,256,384]{2,1,0:T(8,128)(2,1)S(1)}, bf16[2,256,384]{2,1,0:T(8,128)(2,1)}, u32[]{:S(2)}, u32[]{:S(2)}) collective-permute-start(bf16[2,256,384]{2,1,0:T(8,128)(2,1)S(1)} %get-tuple-element.50), channel_id=1, source_target_pairs={{0,1},{1,0},{2,3},{3,2},{4,5},{5,4},{6,7},{7,6},{8,9},{9,8},{10,11... | collective-permute-start | bytes 1179656 | tf_op jit(solution)/shard_map/ppermute | solution.py:31
  105.7 1.1 collective-permute-done.21.refs_3_
  106.8 1.2 copy-done.4
  108.0 0.7 shard_map.71
  108.7 0.6 collective-permute-start.22
  109.3 1.1 add_convert_fusion
  110.6 1.8 %collective-permute-start.23 = (bf16[2,48,1152]{2,1,0:T(8,128)(2,1)S(1)}, bf16[2,48,1152]{2,1,0:T(8,128)(2,1)S(1)}, u32[]{:S(2)}, u32[]{:S(2)}) collective-permute-start(bf16[2,48,1152]{2,1,0:T(8,128)(2,1)S(1)} %get-tuple-element.57), channel_id=1, source_target_pairs={{0,64},{1,193},{2,66},{3,195},{4,68},{5,197},{6,70},{7,199},{8,72}... | collective-permute-start | bytes 663560 | tf_op jit(solution)/shard_map/ppermute | solution.py:31
  112.4 2.3 %collective-permute-done.22 = bf16[2,48,1152]{2,1,0:T(8,128)(2,1)S(1)} collective-permute-done((bf16[2,48,1152]{2,1,0:T(8,128)(2,1)S(1)}, bf16[2,48,1152]{2,1,0:T(8,128)(2,1)S(1)}, u32[]{:S(2)}, u32[]{:S(2)}) %collective-permute-start.22) | collective-permute-done | bytes 221216 | tf_op jit(solution)/shard_map/ppermute | solution.py:31
  114.8 1.8 %collective-permute-done.23 = bf16[2,48,1152]{2,1,0:T(8,128)(2,1)S(1)} collective-permute-done((bf16[2,48,1152]{2,1,0:T(8,128)(2,1)S(1)}, bf16[2,48,1152]{2,1,0:T(8,128)(2,1)S(1)}, u32[]{:S(2)}, u32[]{:S(2)}) %collective-permute-start.23) | collective-permute-done | bytes 221216 | tf_op jit(solution)/shard_map/ppermute | solution.py:31
  116.6 2.6 %collective-permute-done.24 = bf16[256,384]{1,0:T(8,128)(2,1)S(1)} collective-permute-done((bf16[256,384]{1,0:T(8,128)(2,1)S(1)}, bf16[256,384]{1,0:T(8,128)(2,1)S(1)}, u32[]{:S(2)}, u32[]{:S(2)}) %collective-permute-start.24) | collective-permute-done | bytes 196640 | tf_op jit(solution)/shard_map/ppermute | solution.py:31
  119.2 0.1 collective-permute-start.26
  119.4 4.9 %collective-permute-start.19 = (bf16[2,256,384]{2,1,0:T(8,128)(2,1)S(1)}, bf16[2,256,384]{2,1,0:T(8,128)(2,1)S(1)}, u32[]{:S(2)}, u32[]{:S(2)}) collective-permute-start(bf16[2,256,384]{2,1,0:T(8,128)(2,1)S(1)} %pad_maximum_fusion.8), channel_id=1, source_target_pairs={{0,0},{1,1},{2,2},{3,3},{4,4},{5,5},{6,6},{7,7},{8,8},{9,9},{10,10... | collective-permute-start | bytes 1179656 | tf_op jit(solution)/shard_map/ppermute | solution.py:31
  124.4 0.8 collective-permute-done.26
  125.2 5.1 %collective-permute-done.25 = bf16[48,1152]{1,0:T(8,128)(2,1)S(1)} collective-permute-done((bf16[48,1152]{1,0:T(8,128)(2,1)S(1)}, bf16[48,1152]{1,0:T(8,128)(2,1)S(1)}, u32[]{:S(2)}, u32[]{:S(2)}) %collective-permute-start.25) | collective-permute-done | bytes 110624 | tf_op jit(solution)/shard_map/ppermute | solution.py:31
  130.5 0.9 collective-permute-start.29
  131.3 1.2 collective-permute-start.27
  132.6 2.2 %collective-permute-done.19 = bf16[2,256,384]{2,1,0:T(8,128)(2,1)S(1)} collective-permute-done((bf16[2,256,384]{2,1,0:T(8,128)(2,1)S(1)}, bf16[2,256,384]{2,1,0:T(8,128)(2,1)S(1)}, u32[]{:S(2)}, u32[]{:S(2)}) %collective-permute-start.19) | collective-permute-done | bytes 393248 | tf_op jit(solution)/shard_map/ppermute | solution.py:31
  134.7 0.7 fusion.6
  135.5 0.7 slice_bitcast_fusion.3
  136.2 0.9 collective-permute-done.29
  137.1 2.1 %collective-permute-done.28 = bf16[24,1152]{1,0:T(8,128)(2,1)S(1)} collective-permute-done((bf16[24,1152]{1,0:T(8,128)(2,1)S(1)}, bf16[24,1152]{1,0:T(8,128)(2,1)S(1)}, u32[]{:S(2)}, u32[]{:S(2)}) %collective-permute-start.28) | collective-permute-done | bytes 55328 | tf_op jit(solution)/shard_map/ppermute | solution.py:31
  139.2 0.7 pad_maximum_fusion.9
  (82 shorter events, 2.0 us)
Async XLA Ops:
  0.6 15.6 %copy-start = (s32[128,9]{0,1:T(8,128)S(1)}, s32[128,9]{0,1:T(8,128)}, u32[]{:S(2)}) copy-start(s32[128,9]{0,1:T(8,128)} %param.7) | copy-start | bytes 13828
  0.6 18.2 %collective-permute-start = (bf16[256,384]{1,0:T(8,128)(2,1)}, bf16[256,384]{1,0:T(8,128)(2,1)S(1)}, u32[]{:S(2)}, u32[]{:S(2)}) collective-permute-start(bf16[256,384]{1,0:T(8,128)(2,1)} %param.4), channel_id=1, source_target_pairs={{0,0},{1,1},{2,2},{3,3},{4,4},{5,5},{6,6},{7,7},{8,8},{9,9},{10,10... | collective-permute-start | bytes 589832 | tf_op jit(solution)/shard_map/ppermute | solution.py:31
  7.2 11.6 %collective-permute-start.1 = (bf16[256,384]{1,0:T(8,128)(2,1)}, bf16[256,384]{1,0:T(8,128)(2,1)S(1)}, u32[]{:S(2)}, u32[]{:S(2)}) collective-permute-start(bf16[256,384]{1,0:T(8,128)(2,1)} %param.4), channel_id=1, source_target_pairs={{0,2},{1,3},{2,0},{3,1},{4,6},{5,7},{6,4},{7,5},{8,10},{9,11},{10,... | collective-permute-start | bytes 589832 | tf_op jit(solution)/shard_map/ppermute | solution.py:31
  10.4 42.5 %collective-permute-start.3 = (bf16[256,384]{1,0:T(8,128)(2,1)}, bf16[256,384]{1,0:T(8,128)(2,1)S(1)}, u32[]{:S(2)}, u32[]{:S(2)}) collective-permute-start(bf16[256,384]{1,0:T(8,128)(2,1)} %param.6), channel_id=1, source_target_pairs={{0,0},{1,1},{2,2},{3,3},{4,4},{5,5},{6,6},{7,7},{8,8},{9,9},{10,10... | collective-permute-start | bytes 589832 | tf_op jit(solution)/shard_map/ppermute | solution.py:31
  19.6 4.1 %collective-permute-start.2 = (bf16[256,768]{1,0:T(8,128)(2,1)}, bf16[256,768]{1,0:T(8,128)(2,1)S(1)}, u32[]{:S(2)}, u32[]{:S(2)}) collective-permute-start(bf16[256,768]{1,0:T(8,128)(2,1)} %pad_maximum_fusion.7), channel_id=1, source_target_pairs={{0,1},{1,0},{2,3},{3,2},{4,5},{5,4},{6,7},{7,6},{8,9},{9,8},{10,11... | collective-permute-start | bytes 1179656 | tf_op jit(solution)/shard_map/ppermute | solution.py:31
  20.0 13.7 %collective-permute-start.4 = (bf16[256,768]{1,0:T(8,128)(2,1)}, bf16[256,768]{1,0:T(8,128)(2,1)S(1)}, u32[]{:S(2)}, u32[]{:S(2)}) collective-permute-start(bf16[256,768]{1,0:T(8,128)(2,1)} %pad_maximum_fusion.7), channel_id=1, source_target_pairs={{0,4},{1,5},{2,6},{3,7},{4,8},{5,9},{6,10},{7,11},{8,12},{9,13},{1... | collective-permute-start | bytes 1179656 | tf_op jit(solution)/shard_map/ppermute | solution.py:31
  20.0 16.3 %collective-permute-start.8 = (bf16[256,768]{1,0:T(8,128)(2,1)}, bf16[256,768]{1,0:T(8,128)(2,1)S(1)}, u32[]{:S(2)}, u32[]{:S(2)}) collective-permute-start(bf16[256,768]{1,0:T(8,128)(2,1)} %pad_maximum_fusion.7), channel_id=1, source_target_pairs={{0,240},{1,241},{2,242},{3,243},{4,0},{5,1},{6,2},{7,3},{8,4},{9,5... | collective-permute-start | bytes 1179656 | tf_op jit(solution)/shard_map/ppermute | solution.py:31
  33.7 5.3 %collective-permute-start.7 = (bf16[256,768]{1,0:T(8,128)(2,1)S(1)}, bf16[256,768]{1,0:T(8,128)(2,1)S(1)}, u32[]{:S(2)}, u32[]{:S(2)}) collective-permute-start(bf16[256,768]{1,0:T(8,128)(2,1)S(1)} %collective-permute-done.4), channel_id=1, source_target_pairs={{0,1},{1,0},{2,3},{3,2},{4,5},{5,4},{6,7},{7,6},{8,9},{9,8},{10,11... | collective-permute-start | bytes 1179656 | tf_op jit(solution)/shard_map/ppermute | solution.py:31
  33.7 4.5 %copy-start.13 = (bf16[1536,768]{1,0:T(8,128)(2,1)S(1)}, bf16[1536,768]{1,0:T(8,128)(2,1)}, u32[]{:S(2)}) copy-start(bf16[1536,768]{1,0:T(8,128)(2,1)} %pad_maximum_fusion) | copy-start | bytes 7077892
  35.8 11.6 %collective-permute-start.5 = (bf16[256,768]{1,0:T(8,128)(2,1)S(1)}, bf16[256,768]{1,0:T(8,128)(2,1)S(1)}, u32[]{:S(2)}, u32[]{:S(2)}) collective-permute-start(bf16[256,768]{1,0:T(8,128)(2,1)S(1)} %collective-permute-done.4), channel_id=1, source_target_pairs={{0,4},{1,5},{2,6},{3,7},{4,8},{5,9},{6,10},{7,11},{8,12},{9,13},{1... | collective-permute-start | bytes 1179656 | tf_op jit(solution)/shard_map/ppermute | solution.py:31
  36.3 2.8 %collective-permute-start.9 = (bf16[256,768]{1,0:T(8,128)(2,1)S(1)}, bf16[256,768]{1,0:T(8,128)(2,1)S(1)}, u32[]{:S(2)}, u32[]{:S(2)}) collective-permute-start(bf16[256,768]{1,0:T(8,128)(2,1)S(1)} %collective-permute-done.8), channel_id=1, source_target_pairs={{0,1},{1,0},{2,3},{3,2},{4,5},{5,4},{6,7},{7,6},{8,9},{9,8},{10,11... | collective-permute-start | bytes 1179656 | tf_op jit(solution)/shard_map/ppermute | solution.py:31
  36.6 13.4 %collective-permute-start.10 = (bf16[256,768]{1,0:T(8,128)(2,1)S(1)}, bf16[256,768]{1,0:T(8,128)(2,1)S(1)}, u32[]{:S(2)}, u32[]{:S(2)}) collective-permute-start(bf16[256,768]{1,0:T(8,128)(2,1)S(1)} %collective-permute-done.8), channel_id=1, source_target_pairs={{0,240},{1,241},{2,242},{3,243},{4,0},{5,1},{6,2},{7,3},{8,4},{9,5... | collective-permute-start | bytes 1179656 | tf_op jit(solution)/shard_map/ppermute | solution.py:31
  47.4 3.4 %collective-permute-start.6 = (bf16[256,768]{1,0:T(8,128)(2,1)S(1)}, bf16[256,768]{1,0:T(8,128)(2,1)S(1)}, u32[]{:S(2)}, u32[]{:S(2)}) collective-permute-start(bf16[256,768]{1,0:T(8,128)(2,1)S(1)} %collective-permute-done.5), channel_id=1, source_target_pairs={{0,1},{1,0},{2,3},{3,2},{4,5},{5,4},{6,7},{7,6},{8,9},{9,8},{10,11... | collective-permute-start | bytes 1179656 | tf_op jit(solution)/shard_map/ppermute | solution.py:31
  50.0 1.9 %collective-permute-start.11 = (bf16[256,768]{1,0:T(8,128)(2,1)S(1)}, bf16[256,768]{1,0:T(8,128)(2,1)S(1)}, u32[]{:S(2)}, u32[]{:S(2)}) collective-permute-start(bf16[256,768]{1,0:T(8,128)(2,1)S(1)} %collective-permute-done.10), channel_id=1, source_target_pairs={{0,1},{1,0},{2,3},{3,2},{4,5},{5,4},{6,7},{7,6},{8,9},{9,8},{10,11... | collective-permute-start | bytes 1179656 | tf_op jit(solution)/shard_map/ppermute | solution.py:31
  59.1 0.9 copy-start.7
  60.0 0.7 copy-start.11
  60.7 10.2 %copy-start.9 = (bf16[256,384]{1,0:T(8,128)(2,1)}, bf16[256,384]{1,0:T(8,128)(2,1)S(1)}, u32[]{:S(2)}) copy-start(bf16[256,384]{1,0:T(8,128)(2,1)S(1)} %get-tuple-element.35.dq_ref) | copy-start | bytes 589828
  60.7 13.6 %collective-permute-start.14 = (bf16[256,768]{1,0:T(8,128)(2,1)S(1)}, bf16[256,768]{1,0:T(8,128)(2,1)S(1)}, u32[]{:S(2)}, u32[]{:S(2)}) collective-permute-start(bf16[256,768]{1,0:T(8,128)(2,1)S(1)} %get-tuple-element.37.refs_5_), channel_id=1, source_target_pairs={{0,240},{1,241},{2,242},{3,243},{4,0},{5,1},{6,2},{7,3},{8,4},{9,5... | collective-permute-start | bytes 1179656 | tf_op jit(solution)/shard_map/ppermute | solution.py:31
  60.8 14.4 %collective-permute-start.16 = (bf16[256,768]{1,0:T(8,128)(2,1)S(1)}, bf16[256,768]{1,0:T(8,128)(2,1)S(1)}, u32[]{:S(2)}, u32[]{:S(2)}) collective-permute-start(bf16[256,768]{1,0:T(8,128)(2,1)S(1)} %get-tuple-element.41.refs_9_), channel_id=1, source_target_pairs={{0,4},{1,5},{2,6},{3,7},{4,8},{5,9},{6,10},{7,11},{8,12},{9,13},{1... | collective-permute-start | bytes 1179656 | tf_op jit(solution)/shard_map/ppermute | solution.py:31
  70.9 14.8 %copy-start.1 = (bf16[2,4,48,1152]{3,2,1,0:T(8,128)(2,1)S(1)}, bf16[2,4,48,1152]{3,2,1,0:T(8,128)(2,1)}, u32[]{:S(2)}) copy-start(bf16[2,4,48,1152]{3,2,1,0:T(8,128)(2,1)} %get-tuple-element.42.refs_0_) | copy-start | bytes 2654212
  70.9 14.8 %copy-start.2 = (bf16[2,4,48,1152]{3,2,1,0:T(8,128)(2,1)S(1)}, bf16[2,4,48,1152]{3,2,1,0:T(8,128)(2,1)}, u32[]{:S(2)}) copy-start(bf16[2,4,48,1152]{3,2,1,0:T(8,128)(2,1)} %get-tuple-element.43.refs_1_) | copy-start | bytes 2654212
  70.9 13.3 %collective-permute-start.12 = (bf16[2,4,48,1152]{3,2,1,0:T(8,128)(2,1)}, bf16[2,4,48,1152]{3,2,1,0:T(8,128)(2,1)S(1)}, u32[]{:S(2)}, u32[]{:S(2)}) collective-permute-start(bf16[2,4,48,1152]{3,2,1,0:T(8,128)(2,1)} %get-tuple-element.44), channel_id=1, source_target_pairs={{0,64},{1,193},{2,66},{3,195},{4,68},{5,197},{6,70},{7,199},{8,72}... | collective-permute-start | bytes 2654216 | tf_op jit(solution)/shard_map/ppermute | solution.py:31
  72.5 13.3 %collective-permute-start.13 = (bf16[2,4,48,1152]{3,2,1,0:T(8,128)(2,1)}, bf16[2,4,48,1152]{3,2,1,0:T(8,128)(2,1)S(1)}, u32[]{:S(2)}, u32[]{:S(2)}) collective-permute-start(bf16[2,4,48,1152]{3,2,1,0:T(8,128)(2,1)} %get-tuple-element.45), channel_id=1, source_target_pairs={{0,16},{1,49},{2,18},{3,51},{4,20},{5,53},{6,22},{7,55},{8,24},{9,... | collective-permute-start | bytes 2654216 | tf_op jit(solution)/shard_map/ppermute | solution.py:31
  75.2 22.0 %collective-permute-start.15 = (bf16[256,768]{1,0:T(8,128)(2,1)}, bf16[256,768]{1,0:T(8,128)(2,1)}, u32[]{:S(2)}, u32[]{:S(2)}) collective-permute-start(bf16[256,768]{1,0:T(8,128)(2,1)} %add_convert_fusion.2), channel_id=1, source_target_pairs={{0,240},{1,241},{2,242},{3,243},{4,0},{5,1},{6,2},{7,3},{8,4},{9,5... | collective-permute-start | bytes 1179656 | tf_op jit(solution)/shard_map/ppermute | solution.py:31
  76.1 21.1 %collective-permute-start.17 = (bf16[256,768]{1,0:T(8,128)(2,1)}, bf16[256,768]{1,0:T(8,128)(2,1)}, u32[]{:S(2)}, u32[]{:S(2)}) collective-permute-start(bf16[256,768]{1,0:T(8,128)(2,1)} %add_convert_fusion.1), channel_id=1, source_target_pairs={{0,4},{1,5},{2,6},{3,7},{4,8},{5,9},{6,10},{7,11},{8,12},{9,13},{1... | collective-permute-start | bytes 1179656 | tf_op jit(solution)/shard_map/ppermute | solution.py:31
  85.8 11.4 %copy-start.8 = (f32[256,768]{1,0:T(8,128)S(1)}, f32[256,768]{1,0:T(8,128)}, u32[]{:S(2)}) copy-start(f32[256,768]{1,0:T(8,128)} %copy-done.7) | copy-start | bytes 2359300
  85.8 11.4 %copy-start.10 = (bf16[256,384]{1,0:T(8,128)(2,1)S(1)}, bf16[256,384]{1,0:T(8,128)(2,1)}, u32[]{:S(2)}) copy-start(bf16[256,384]{1,0:T(8,128)(2,1)} %copy-done.9) | copy-start | bytes 589828
  87.0 0.9 copy-start.5
  87.9 13.3 %copy-start.3 = (f32[4,48,1152]{2,1,0:T(8,128)}, f32[4,48,1152]{2,1,0:T(8,128)S(1)}, u32[]{:S(2)}) copy-start(f32[4,48,1152]{2,1,0:T(8,128)S(1)} %get-tuple-element.51.refs_0_) | copy-start | bytes 2654212
  87.9 17.8 %collective-permute-start.20 = (bf16[4,48,1152]{2,1,0:T(8,128)(2,1)}, bf16[4,48,1152]{2,1,0:T(8,128)(2,1)S(1)}, u32[]{:S(2)}, u32[]{:S(2)}) collective-permute-start(bf16[4,48,1152]{2,1,0:T(8,128)(2,1)} %get-tuple-element.46), channel_id=1, source_target_pairs={{0,192},{1,65},{2,194},{3,67},{4,196},{5,69},{6,198},{7,71},{8,200... | collective-permute-start | bytes 1327112 | tf_op jit(solution)/shard_map/ppermute | solution.py:31
  97.1 9.7 %collective-permute-start.21 = (bf16[4,48,1152]{2,1,0:T(8,128)(2,1)}, bf16[4,48,1152]{2,1,0:T(8,128)(2,1)S(1)}, u32[]{:S(2)}, u32[]{:S(2)}) collective-permute-start(bf16[4,48,1152]{2,1,0:T(8,128)(2,1)} %get-tuple-element.53), channel_id=1, source_target_pairs={{0,48},{1,17},{2,50},{3,19},{4,52},{5,21},{6,54},{7,23},{8,56},{9,... | collective-permute-start | bytes 1327112 | tf_op jit(solution)/shard_map/ppermute | solution.py:31
  97.2 9.6 %copy-start.6 = (f32[4,48,1152]{2,1,0:T(8,128)S(1)}, f32[4,48,1152]{2,1,0:T(8,128)}, u32[]{:S(2)}) copy-start(f32[4,48,1152]{2,1,0:T(8,128)} %copy-done.5) | copy-start | bytes 2654212
  101.2 8.0 %collective-permute-start.18 = (bf16[2,256,384]{2,1,0:T(8,128)(2,1)S(1)}, bf16[2,256,384]{2,1,0:T(8,128)(2,1)}, u32[]{:S(2)}, u32[]{:S(2)}) collective-permute-start(bf16[2,256,384]{2,1,0:T(8,128)(2,1)S(1)} %get-tuple-element.50), channel_id=1, source_target_pairs={{0,1},{1,0},{2,3},{3,2},{4,5},{5,4},{6,7},{7,6},{8,9},{9,8},{10,11... | collective-permute-start | bytes 1179656 | tf_op jit(solution)/shard_map/ppermute | solution.py:31
  106.8 1.2 copy-start.4
  108.7 6.0 %collective-permute-start.22 = (bf16[2,48,1152]{2,1,0:T(8,128)(2,1)S(1)}, bf16[2,48,1152]{2,1,0:T(8,128)(2,1)S(1)}, u32[]{:S(2)}, u32[]{:S(2)}) collective-permute-start(bf16[2,48,1152]{2,1,0:T(8,128)(2,1)S(1)} %get-tuple-element.55), channel_id=1, source_target_pairs={{0,16},{1,49},{2,18},{3,51},{4,20},{5,53},{6,22},{7,55},{8,24},{9,... | collective-permute-start | bytes 663560 | tf_op jit(solution)/shard_map/ppermute | solution.py:31
  109.3 10.0 %copy-start.12 = (bf16[256,384]{1,0:T(8,128)(2,1)S(1)}, bf16[256,384]{1,0:T(8,128)(2,1)}, u32[]{:S(2)}) copy-start(bf16[256,384]{1,0:T(8,128)(2,1)} %copy-done.11) | copy-start | bytes 589828
  110.5 8.7 %collective-permute-start.24 = (bf16[256,384]{1,0:T(8,128)(2,1)S(1)}, bf16[256,384]{1,0:T(8,128)(2,1)S(1)}, u32[]{:S(2)}, u32[]{:S(2)}) collective-permute-start(bf16[256,384]{1,0:T(8,128)(2,1)S(1)} %get-tuple-element.76), channel_id=1, source_target_pairs={{0,2},{1,3},{2,0},{3,1},{4,6},{5,7},{6,4},{7,5},{8,10},{9,11},{10,... | collective-permute-start | bytes 589832 | tf_op jit(solution)/shard_map/ppermute | solution.py:31
  110.6 6.0 %collective-permute-start.23 = (bf16[2,48,1152]{2,1,0:T(8,128)(2,1)S(1)}, bf16[2,48,1152]{2,1,0:T(8,128)(2,1)S(1)}, u32[]{:S(2)}, u32[]{:S(2)}) collective-permute-start(bf16[2,48,1152]{2,1,0:T(8,128)(2,1)S(1)} %get-tuple-element.57), channel_id=1, source_target_pairs={{0,64},{1,193},{2,66},{3,195},{4,68},{5,197},{6,70},{7,199},{8,72}... | collective-permute-start | bytes 663560 | tf_op jit(solution)/shard_map/ppermute | solution.py:31
  119.2 6.0 %collective-permute-start.26 = (bf16[48,1152]{1,0:T(8,128)(2,1)S(1)}, bf16[48,1152]{1,0:T(8,128)(2,1)S(1)}, u32[]{:S(2)}, u32[]{:S(2)}) collective-permute-start(bf16[48,1152]{1,0:T(8,128)(2,1)S(1)} %fusion.8), channel_id=1, source_target_pairs={{0,192},{1,65},{2,194},{3,67},{4,196},{5,69},{6,198},{7,71},{8,200... | collective-permute-start | bytes 331784 | tf_op jit(solution)/shard_map/ppermute | solution.py:31
  119.4 15.4 %collective-permute-start.19 = (bf16[2,256,384]{2,1,0:T(8,128)(2,1)S(1)}, bf16[2,256,384]{2,1,0:T(8,128)(2,1)S(1)}, u32[]{:S(2)}, u32[]{:S(2)}) collective-permute-start(bf16[2,256,384]{2,1,0:T(8,128)(2,1)S(1)} %pad_maximum_fusion.8), channel_id=1, source_target_pairs={{0,0},{1,1},{2,2},{3,3},{4,4},{5,5},{6,6},{7,7},{8,8},{9,9},{10,10... | collective-permute-start | bytes 1179656 | tf_op jit(solution)/shard_map/ppermute | solution.py:31
  124.3 6.0 %collective-permute-start.25 = (bf16[48,1152]{1,0:T(8,128)(2,1)S(1)}, bf16[48,1152]{1,0:T(8,128)(2,1)S(1)}, u32[]{:S(2)}, u32[]{:S(2)}) collective-permute-start(bf16[48,1152]{1,0:T(8,128)(2,1)S(1)} %fusion.7), channel_id=1, source_target_pairs={{0,48},{1,17},{2,50},{3,19},{4,52},{5,21},{6,54},{7,23},{8,56},{9,... | collective-permute-start | bytes 331784 | tf_op jit(solution)/shard_map/ppermute | solution.py:31
  130.5 6.6 %collective-permute-start.29 = (bf16[24,1152]{1,0:T(8,128)(2,1)S(1)}, bf16[24,1152]{1,0:T(8,128)(2,1)S(1)}, u32[]{:S(2)}, u32[]{:S(2)}) collective-permute-start(bf16[24,1152]{1,0:T(8,128)(2,1)S(1)} %get-tuple-element.74), channel_id=1, source_target_pairs={{0,12},{1,13},{2,14},{3,15},{4,0},{5,1},{6,2},{7,3},{8,4},{9,5},{1... | collective-permute-start | bytes 165896 | tf_op jit(solution)/shard_map/ppermute | solution.py:31
  131.3 7.8 %collective-permute-start.28 = (bf16[24,1152]{1,0:T(8,128)(2,1)S(1)}, bf16[24,1152]{1,0:T(8,128)(2,1)S(1)}, u32[]{:S(2)}, u32[]{:S(2)}) collective-permute-start(bf16[24,1152]{1,0:T(8,128)(2,1)S(1)} %get-tuple-element.75), channel_id=1, source_target_pairs={{0,8},{1,9},{2,10},{3,11},{4,12},{5,13},{6,14},{7,15},{8,0},{9,1},... | collective-permute-start | bytes 165896 | tf_op jit(solution)/shard_map/ppermute | solution.py:31
  131.3 7.8 %collective-permute-start.27 = (bf16[24,1152]{1,0:T(8,128)(2,1)S(1)}, bf16[24,1152]{1,0:T(8,128)(2,1)S(1)}, u32[]{:S(2)}, u32[]{:S(2)}) collective-permute-start(bf16[24,1152]{1,0:T(8,128)(2,1)S(1)} %get-tuple-element.73), channel_id=1, source_target_pairs={{0,4},{1,5},{2,6},{3,7},{4,8},{5,9},{6,10},{7,11},{8,12},{9,13},{1... | collective-permute-start | bytes 165896 | tf_op jit(solution)/shard_map/ppermute | solution.py:31

commit v2 on v1

--- a/solution.py
+++ b/solution.py
@@ -122,7 +122,7 @@
         + [jax.ShapeDtypeStruct((rows, 2 * width), BF16)] * SLABS,
         in_specs=[pl.BlockSpec(memory_space=pltpu.VMEM)] * (3 + SLABS),
         out_specs=[pl.BlockSpec(memory_space=pltpu.VMEM)] * (3 + SLABS),
-        compiler_params=pltpu.CompilerParams(vmem_limit_bytes=40 * 1024 * 1024),
+        compiler_params=pltpu.CompilerParams(vmem_limit_bytes=48 * 1024 * 1024),
         cost_estimate=pl.CostEstimate(
             flops=12 * rows * SLABS * rows * width,
             bytes_accessed=20 * rows * width * 2,
@@ -322,10 +322,11 @@
         return dot(tokens, weight_kv, NN).astype(BF16)
 
     mine = [None, along_chain(pair, 1), pair, along_chain(pair, -1), None]
+    whole = full(pair, swapped(pair))
+    queries = dot(whole, weight_q, NN).astype(BF16)
+    mine[1], mine[3], queries = lax.optimization_barrier((mine[1], mine[3], queries))
     mine[0], mine[4] = along_chain(mine[1], 1), along_chain(mine[3], -1)
-    tokens = [full(v, swapped(v)) for v in mine]
-    whole = tokens[REACH]
-    queries = dot(whole, weight_q, NN).astype(BF16)
+    tokens = [whole if w == REACH else full(v, swapped(v)) for w, v in enumerate(mine)]
     slabs = [keys_values(t) for t in tokens]
     grad_out = reversal(out_grad)
 

time: 140 us -> 136 us (0.971)
  waiting for transfers between devices: 46.3 us -> 43.8 us
  local copies, waits for them, and re-layouts: 7.16 us -> 5.57 us
    ppermute x30, waiting for transfers between devices: 46.3 us -> 43.8 us  [move(): lax.ppermute(value, AXES, [(i, flat(*to(*coords(i)))) for i in range(256)])]
    unnamed x30, local copies, waits for them, and re-layouts: 3.69 us -> 2.16 us
  transfers between devices with their start and end apart: 30 -> 30, of which waited for: 16 -> 17; matrix products, arithmetic and copies ran while one was open for 12% -> 12% of each run, Pallas kernels for 9% -> 9%
where the time goes in v2:
time: 136 us; the launch traced here: 135 us
  starting transfers between devices  53.3 us (39%)
  waiting for transfers between devices  43.8 us (32%)
  Pallas kernels  18.3 us (13%)
  other arithmetic  7.22 us (5%)
  matrix products  5.89 us (4%)
  local copies, waits for them, and re-layouts  5.57 us (4%)
    ppermute x30, starting transfers between devices, move(): lax.ppermute(value, AXES, [(i, flat(*to(*coords(i)))) for i in range(256)])  53.3 us
    ppermute x30, waiting for transfers between devices, move(): lax.ppermute(value, AXES, [(i, flat(*to(*coords(i)))) for i in range(256)])  43.8 us
    pallas_call x1, Pallas kernels, attention(): pl.pallas_call(attention_kernel, out_shape=[jax.ShapeDtypeStruct((rows, w...  6.21 us
    pallas_call x1, Pallas kernels, weight_terms(): pl.pallas_call(weight_kernel, out_shape=[jax.ShapeDtypeStruct(shape, BF16...  6.1 us
    dot_general x6, matrix products, dot(): return lax.dot_general(a, b, dims, preferred_element_type=F32)  5.89 us
    pallas_call x1, Pallas kernels, input_terms(): pl.pallas_call(input_kernel, out_shape=[jax.ShapeDtypeStruct((2, rows, wi...  4.03 us
  transfers between devices with their start and end apart: 30, of which 17 were waited for; matrix products, arithmetic and copies ran while one was open for 12% of the time, Pallas kernels for 9%

profile of v2, /device:TPU:24, one launch (start us, length us, event | category | flops | bytes accessed | tf_op | source)
XLA Modules:
  0.0 135.4 jit_solution(9944426183646350631)
XLA Ops:
  0.6 6.5 %collective-permute-start = (bf16[256,384]{1,0:T(8,128)(2,1)}, bf16[256,384]{1,0:T(8,128)(2,1)S(1)}, u32[]{:S(2)}, u32[]{:S(2)}) collective-permute-start(bf16[256,384]{1,0:T(8,128)(2,1)} %param.4), channel_id=1, source_target_pairs={{0,0},{1,1},{2,2},{3,3},{4,4},{5,5},{6,6},{7,7},{8,8},{9,9},{10,10... | collective-permute-start | bytes 589832 | tf_op jit(solution)/shard_map/ppermute | solution.py:31
  7.2 3.2 %collective-permute-start.1 = (bf16[256,384]{1,0:T(8,128)(2,1)}, bf16[256,384]{1,0:T(8,128)(2,1)S(1)}, u32[]{:S(2)}, u32[]{:S(2)}) collective-permute-start(bf16[256,384]{1,0:T(8,128)(2,1)} %param.4), channel_id=1, source_target_pairs={{0,2},{1,3},{2,0},{3,1},{4,6},{5,7},{6,4},{7,5},{8,10},{9,11},{10,... | collective-permute-start | bytes 589832 | tf_op jit(solution)/shard_map/ppermute | solution.py:31
  10.4 3.8 %collective-permute-start.5 = (bf16[256,384]{1,0:T(8,128)(2,1)}, bf16[256,384]{1,0:T(8,128)(2,1)S(1)}, u32[]{:S(2)}, u32[]{:S(2)}) collective-permute-start(bf16[256,384]{1,0:T(8,128)(2,1)} %param.6), channel_id=1, source_target_pairs={{0,0},{1,1},{2,2},{3,3},{4,4},{5,5},{6,6},{7,7},{8,8},{9,9},{10,10... | collective-permute-start | bytes 589832 | tf_op jit(solution)/shard_map/ppermute | solution.py:31
  14.3 1.9 %slice_bitcast_fusion.1 = (bf16[1536,384]{1,0:T(8,128)(2,1)S(1)}, bf16[1536,384]{1,0:T(8,128)(2,1)S(1)}) fusion(bf16[3,1536,384]{2,1,0:T(8,128)(2,1)} %weight_ref.1), kind=kLoop, calls=%fused_computation.10 | loop fusion | bytes 4718592 | tf_op jit(solution)/shard_map/squeeze | solution.py:308
  16.3 0.1 copy.8
  16.4 1.6 %pad_maximum_fusion = bf16[1536,768]{1,0:T(8,128)(2,1)} fusion(bf16[1536,384]{1,0:T(8,128)(2,1)S(1)} %get-tuple-element.68, bf16[1536,384]{1,0:T(8,128)(2,1)S(1)} %get-tuple-element.67), kind=kLoop, calls=%fused_computation | loop fusion | flops 4718592 | bytes 4718592 | tf_op jit(solution)/shard_map/concatenate | solution.py:308
  18.0 0.2 compare_reduce_fusion
  18.2 0.6 collective-permute-done.1
  18.9 0.1 collective-permute-start.4
  19.0 0.1 copy.9
  19.4 3.7 %collective-permute-start.3 = (bf16[256,768]{1,0:T(8,128)(2,1)S(1)}, bf16[256,768]{1,0:T(8,128)(2,1)S(1)}, u32[]{:S(2)}, u32[]{:S(2)}) collective-permute-start(bf16[256,768]{1,0:T(8,128)(2,1)S(1)} %pad_maximum_fusion.7), channel_id=1, source_target_pairs={{0,240},{1,241},{2,242},{3,243},{4,0},{5,1},{6,2},{7,3},{8,4},{9,5... | collective-permute-start | bytes 1179656 | tf_op jit(solution)/shard_map/ppermute | solution.py:31
  23.1 0.1 broadcast_select_fusion.9
  23.4 2.0 %fusion.3.q_ref = bf16[256,384]{1,0:T(8,128)(2,1)S(1)} fusion(bf16[3,1536,384]{2,1,0:T(8,128)(2,1)} %weight_ref.1, bf16[256,384]{1,0:T(8,128)(2,1)S(1)} %get-tuple-element.111, bf16[256,384]{1,0:T(8,128)(2,1)S(1)} %get-tuple-element.101, bf16[256,384]{1,0:T(8,128)(2,1)S(1)} %get-tuple-element.112, bf16[256,384]{1,0:T(8,128)(2,1)S(1)} %get-tuple-element.100), kind=kOutput, calls=%fused_computation.11 | convolution fusion | flops 305233920 | bytes 2162688 | tf_op jit(solution)/shard_map/dot_general | solution.py:64
  25.4 7.4 %collective-permute-done.2 = bf16[256,768]{1,0:T(8,128)(2,1)S(1)} collective-permute-done((bf16[256,768]{1,0:T(8,128)(2,1)S(1)}, bf16[256,768]{1,0:T(8,128)(2,1)S(1)}, u32[]{:S(2)}, u32[]{:S(2)}) %collective-permute-start.2) | collective-permute-done | bytes 393248 | tf_op jit(solution)/shard_map/ppermute | solution.py:31
  32.8 0.3 collective-permute-done.3
  33.1 0.2 collective-permute-start.6
  33.3 0.5 collective-permute-start.9
  33.8 1.8 %collective-permute-start.10 = (bf16[256,768]{1,0:T(8,128)(2,1)S(1)}, bf16[256,768]{1,0:T(8,128)(2,1)S(1)}, u32[]{:S(2)}, u32[]{:S(2)}) collective-permute-start(bf16[256,768]{1,0:T(8,128)(2,1)S(1)} %collective-permute-done.3), channel_id=1, source_target_pairs={{0,240},{1,241},{2,242},{3,243},{4,0},{5,1},{6,2},{7,3},{8,4},{9,5... | collective-permute-start | bytes 1179656 | tf_op jit(solution)/shard_map/ppermute | solution.py:31
  35.7 0.8 convolution_convert_fusion.2.refs_2_
  36.9 0.8 convolution_convert_fusion.3.refs_1_
  37.7 6.2 %collective-permute-done.6 = bf16[256,768]{1,0:T(8,128)(2,1)S(1)} collective-permute-done((bf16[256,768]{1,0:T(8,128)(2,1)S(1)}, bf16[256,768]{1,0:T(8,128)(2,1)S(1)}, u32[]{:S(2)}, u32[]{:S(2)}) %collective-permute-start.6) | collective-permute-done | bytes 393248 | tf_op jit(solution)/shard_map/ppermute | solution.py:31
  44.0 3.0 %collective-permute-done.10 = bf16[256,768]{1,0:T(8,128)(2,1)S(1)} collective-permute-done((bf16[256,768]{1,0:T(8,128)(2,1)S(1)}, bf16[256,768]{1,0:T(8,128)(2,1)S(1)}, u32[]{:S(2)}, u32[]{:S(2)}) %collective-permute-start.10) | collective-permute-done | bytes 393248 | tf_op jit(solution)/shard_map/ppermute | solution.py:31
  46.9 0.8 convolution_convert_fusion.1.refs_3_
  48.0 0.8 convolution_convert_fusion.4.refs_0_
  48.9 0.8 convolution_convert_fusion.refs_4_
  49.8 6.2 %shard_map.67 = (bf16[256,384]{1,0:T(8,128)(2,1)S(1)}, bf16[256,384]{1,0:T(8,128)(2,1)S(1)}, f32[256,768]{1,0:T(8,128)S(1)}, bf16[256,768]{1,0:T(8,128)(2,1)S(1)...) custom-call(bf16[256,384]{1,0:T(8,128)(2,1)S(1)} %fusion.3.q_ref, ...), custom_call_target="tpu_custom_call" | custom-call | flops 1509949440 | bytes 3932160 | tf_op jit(solution)/shard_map/pallas_call | solution.py:115
  56.1 0.1 collective-permute-start.14
  56.1 4.1 %collective-permute-start.16 = (bf16[256,768]{1,0:T(8,128)(2,1)S(1)}, bf16[256,768]{1,0:T(8,128)(2,1)S(1)}, u32[]{:S(2)}, u32[]{:S(2)}) collective-permute-start(bf16[256,768]{1,0:T(8,128)(2,1)S(1)} %get-tuple-element.47.refs_9_), channel_id=1, source_target_pairs={{0,4},{1,5},{2,6},{3,7},{4,8},{5,9},{6,10},{7,11},{8,12},{9,13},{1... | collective-permute-start | bytes 1179656 | tf_op jit(solution)/shard_map/ppermute | solution.py:31
  60.3 6.1 %shard_map.68 = (bf16[2,4,48,1152]{3,2,1,0:T(8,128)(2,1)}, bf16[2,4,48,1152]{3,2,1,0:T(8,128)(2,1)}, bf16[2,4,48,1152]{3,2,1,0:T(8,128)(2,1)}, bf16[2,4,48,1152]{3,2,1,0:T(8,128)(2,1)}) custom-call(s32[2,4]{1,0:T(2,128)S(1)} %pad_add_fusion.order_ref, bf16[256,384]{1,0:T(8,128)(2,1)S(1)} %get-tuple-element.41.dq_ref, ...), custom_call_target="tpu_custom_call" | custom-call | flops 3300000000 | bytes 30000000 | tf_op jit(solution)/shard_map/pallas_call | solution.py:171
  66.4 1.6 %collective-permute-start.12 = (bf16[2,4,48,1152]{3,2,1,0:T(8,128)(2,1)}, bf16[2,4,48,1152]{3,2,1,0:T(8,128)(2,1)S(1)}, u32[]{:S(2)}, u32[]{:S(2)}) collective-permute-start(bf16[2,4,48,1152]{3,2,1,0:T(8,128)(2,1)} %get-tuple-element.50), channel_id=1, source_target_pairs={{0,64},{1,193},{2,66},{3,195},{4,68},{5,197},{6,70},{7,199},{8,72}... | collective-permute-start | bytes 2654216 | tf_op jit(solution)/shard_map/ppermute | solution.py:31
  68.0 1.8 %collective-permute-done.14 = bf16[256,768]{1,0:T(8,128)(2,1)S(1)} collective-permute-done((bf16[256,768]{1,0:T(8,128)(2,1)S(1)}, bf16[256,768]{1,0:T(8,128)(2,1)S(1)}, u32[]{:S(2)}, u32[]{:S(2)}) %collective-permute-start.14) | collective-permute-done | bytes 393248 | tf_op jit(solution)/shard_map/ppermute | solution.py:31
  69.8 0.9 add_convert_fusion.2
  70.6 0.9 add_convert_fusion.1
  71.5 4.1 %collective-permute-start.17 = (bf16[256,768]{1,0:T(8,128)(2,1)}, bf16[256,768]{1,0:T(8,128)(2,1)}, u32[]{:S(2)}, u32[]{:S(2)}) collective-permute-start(bf16[256,768]{1,0:T(8,128)(2,1)} %add_convert_fusion.1), channel_id=1, source_target_pairs={{0,4},{1,5},{2,6},{3,7},{4,8},{5,9},{6,10},{7,11},{8,12},{9,13},{1... | collective-permute-start | bytes 1179656 | tf_op jit(solution)/shard_map/ppermute | solution.py:31
  75.6 4.1 %collective-permute-done.12.refs_2_ = bf16[2,4,48,1152]{3,2,1,0:T(8,128)(2,1)S(1)} collective-permute-done((bf16[2,4,48,1152]{3,2,1,0:T(8,128)(2,1)}, bf16[2,4,48,1152]{3,2,1,0:T(8,128)(2,1)S(1)}, u32[]{:S(2)}, u32[]{:S(2)}) %collective-permute-start.12) | collective-permute-done | bytes 884768 | tf_op jit(solution)/shard_map/ppermute | solution.py:31
  79.7 1.5 %collective-permute-done.13.refs_3_ = bf16[2,4,48,1152]{3,2,1,0:T(8,128)(2,1)S(1)} collective-permute-done((bf16[2,4,48,1152]{3,2,1,0:T(8,128)(2,1)}, bf16[2,4,48,1152]{3,2,1,0:T(8,128)(2,1)S(1)}, u32[]{:S(2)}, u32[]{:S(2)}) %collective-permute-start.13) | collective-permute-done | bytes 884768 | tf_op jit(solution)/shard_map/ppermute | solution.py:31
  81.2 1.2 shard_map.69
  82.5 0.9 copy-done.5
  83.4 9.1 %collective-permute-start.20 = (bf16[4,48,1152]{2,1,0:T(8,128)(2,1)}, bf16[4,48,1152]{2,1,0:T(8,128)(2,1)S(1)}, u32[]{:S(2)}, u32[]{:S(2)}) collective-permute-start(bf16[4,48,1152]{2,1,0:T(8,128)(2,1)} %get-tuple-element.52), channel_id=1, source_target_pairs={{0,192},{1,65},{2,194},{3,67},{4,196},{5,69},{6,198},{7,71},{8,200... | collective-permute-start | bytes 1327112 | tf_op jit(solution)/shard_map/ppermute | solution.py:31
  92.6 4.0 %shard_map.70 = (bf16[2,256,384]{2,1,0:T(8,128)(2,1)S(1)}, f32[2,256,384]{2,1,0:T(8,128)S(1)}) custom-call(s32[4]{0:T(128)S(1)} %pad_add_fusion.1.place_ref, bf16[256,384]{1,0:T(8,128)(2,1)S(1)} %copy-done.10, f32[256,768]{1,0:T(8,128)S(1)} %copy-done.8, bf16[3,1536,384]{2,1,0:T(8,128)(2,1)} %weight_ref.1, bf16[256,768]{1,0:T(8,128)(2,1)} %collective-permute-done.15.refs_0_, ...), custom_call_target="tpu_custom_call" | custom-call | tf_op jit(solution)/shard_map/pallas_call | solution.py:246
  96.7 4.5 %collective-permute-start.18 = (bf16[2,256,384]{2,1,0:T(8,128)(2,1)S(1)}, bf16[2,256,384]{2,1,0:T(8,128)(2,1)}, u32[]{:S(2)}, u32[]{:S(2)}) collective-permute-start(bf16[2,256,384]{2,1,0:T(8,128)(2,1)S(1)} %get-tuple-element.56), channel_id=1, source_target_pairs={{0,1},{1,0},{2,3},{3,2},{4,5},{5,4},{6,7},{7,6},{8,9},{9,8},{10,11... | collective-permute-start | bytes 1179656 | tf_op jit(solution)/shard_map/ppermute | solution.py:31
  101.2 1.1 collective-permute-done.21.refs_3_
  102.3 1.2 copy-done.4
  103.4 0.7 shard_map.71
  104.1 0.6 collective-permute-start.22
  104.7 1.1 add_convert_fusion
  105.9 0.1 collective-permute-start.24
  106.0 1.8 %collective-permute-start.23 = (bf16[2,48,1152]{2,1,0:T(8,128)(2,1)S(1)}, bf16[2,48,1152]{2,1,0:T(8,128)(2,1)S(1)}, u32[]{:S(2)}, u32[]{:S(2)}) collective-permute-start(bf16[2,48,1152]{2,1,0:T(8,128)(2,1)S(1)} %get-tuple-element.63), channel_id=1, source_target_pairs={{0,64},{1,193},{2,66},{3,195},{4,68},{5,197},{6,70},{7,199},{8,72}... | collective-permute-start | bytes 663560 | tf_op jit(solution)/shard_map/ppermute | solution.py:31
  107.9 2.3 %collective-permute-done.22 = bf16[2,48,1152]{2,1,0:T(8,128)(2,1)S(1)} collective-permute-done((bf16[2,48,1152]{2,1,0:T(8,128)(2,1)S(1)}, bf16[2,48,1152]{2,1,0:T(8,128)(2,1)S(1)}, u32[]{:S(2)}, u32[]{:S(2)}) %collective-permute-start.22) | collective-permute-done | bytes 221216 | tf_op jit(solution)/shard_map/ppermute | solution.py:31
  110.2 1.9 %collective-permute-done.23 = bf16[2,48,1152]{2,1,0:T(8,128)(2,1)S(1)} collective-permute-done((bf16[2,48,1152]{2,1,0:T(8,128)(2,1)S(1)}, bf16[2,48,1152]{2,1,0:T(8,128)(2,1)S(1)}, u32[]{:S(2)}, u32[]{:S(2)}) %collective-permute-start.23) | collective-permute-done | bytes 221216 | tf_op jit(solution)/shard_map/ppermute | solution.py:31
  112.1 2.6 %collective-permute-done.24 = bf16[256,384]{1,0:T(8,128)(2,1)S(1)} collective-permute-done((bf16[256,384]{1,0:T(8,128)(2,1)S(1)}, bf16[256,384]{1,0:T(8,128)(2,1)S(1)}, u32[]{:S(2)}, u32[]{:S(2)}) %collective-permute-start.24) | collective-permute-done | bytes 196640 | tf_op jit(solution)/shard_map/ppermute | solution.py:31
  114.7 0.1 collective-permute-start.26
  114.8 4.9 %collective-permute-start.19 = (bf16[2,256,384]{2,1,0:T(8,128)(2,1)S(1)}, bf16[2,256,384]{2,1,0:T(8,128)(2,1)S(1)}, u32[]{:S(2)}, u32[]{:S(2)}) collective-permute-start(bf16[2,256,384]{2,1,0:T(8,128)(2,1)S(1)} %pad_maximum_fusion.8), channel_id=1, source_target_pairs={{0,0},{1,1},{2,2},{3,3},{4,4},{5,5},{6,6},{7,7},{8,8},{9,9},{10,10... | collective-permute-start | bytes 1179656 | tf_op jit(solution)/shard_map/ppermute | solution.py:31
  119.7 0.1 collective-permute-start.25
  119.8 0.8 collective-permute-done.26
  120.7 5.1 %collective-permute-done.25 = bf16[48,1152]{1,0:T(8,128)(2,1)S(1)} collective-permute-done((bf16[48,1152]{1,0:T(8,128)(2,1)S(1)}, bf16[48,1152]{1,0:T(8,128)(2,1)S(1)}, u32[]{:S(2)}, u32[]{:S(2)}) %collective-permute-start.25) | collective-permute-done | bytes 110624 | tf_op jit(solution)/shard_map/ppermute | solution.py:31
  125.9 0.9 collective-permute-start.29
  126.8 1.2 collective-permute-start.27
  128.0 2.2 %collective-permute-done.19 = bf16[2,256,384]{2,1,0:T(8,128)(2,1)S(1)} collective-permute-done((bf16[2,256,384]{2,1,0:T(8,128)(2,1)S(1)}, bf16[2,256,384]{2,1,0:T(8,128)(2,1)S(1)}, u32[]{:S(2)}, u32[]{:S(2)}) %collective-permute-start.19) | collective-permute-done | bytes 393248 | tf_op jit(solution)/shard_map/ppermute | solution.py:31
  130.2 0.7 fusion.6
  130.9 0.7 slice_bitcast_fusion.3
  131.6 0.9 collective-permute-done.29
  132.5 2.2 %collective-permute-done.28 = bf16[24,1152]{1,0:T(8,128)(2,1)S(1)} collective-permute-done((bf16[24,1152]{1,0:T(8,128)(2,1)S(1)}, bf16[24,1152]{1,0:T(8,128)(2,1)S(1)}, u32[]{:S(2)}, u32[]{:S(2)}) %collective-permute-start.28) | collective-permute-done | bytes 55328 | tf_op jit(solution)/shard_map/ppermute | solution.py:31
  134.7 0.7 pad_maximum_fusion.9
  (86 shorter events, 1.9 us)
Async XLA Ops:
  0.6 15.6 %copy-start = (s32[128,9]{0,1:T(8,128)S(1)}, s32[128,9]{0,1:T(8,128)}, u32[]{:S(2)}) copy-start(s32[128,9]{0,1:T(8,128)} %param.7) | copy-start | bytes 13828
  0.6 18.2 %collective-permute-start = (bf16[256,384]{1,0:T(8,128)(2,1)}, bf16[256,384]{1,0:T(8,128)(2,1)S(1)}, u32[]{:S(2)}, u32[]{:S(2)}) collective-permute-start(bf16[256,384]{1,0:T(8,128)(2,1)} %param.4), channel_id=1, source_target_pairs={{0,0},{1,1},{2,2},{3,3},{4,4},{5,5},{6,6},{7,7},{8,8},{9,9},{10,10... | collective-permute-start | bytes 589832 | tf_op jit(solution)/shard_map/ppermute | solution.py:31
  7.2 11.6 %collective-permute-start.1 = (bf16[256,384]{1,0:T(8,128)(2,1)}, bf16[256,384]{1,0:T(8,128)(2,1)S(1)}, u32[]{:S(2)}, u32[]{:S(2)}) collective-permute-start(bf16[256,384]{1,0:T(8,128)(2,1)} %param.4), channel_id=1, source_target_pairs={{0,2},{1,3},{2,0},{3,1},{4,6},{5,7},{6,4},{7,5},{8,10},{9,11},{10,... | collective-permute-start | bytes 589832 | tf_op jit(solution)/shard_map/ppermute | solution.py:31
  10.4 39.4 %collective-permute-start.5 = (bf16[256,384]{1,0:T(8,128)(2,1)}, bf16[256,384]{1,0:T(8,128)(2,1)S(1)}, u32[]{:S(2)}, u32[]{:S(2)}) collective-permute-start(bf16[256,384]{1,0:T(8,128)(2,1)} %param.6), channel_id=1, source_target_pairs={{0,0},{1,1},{2,2},{3,3},{4,4},{5,5},{6,6},{7,7},{8,8},{9,9},{10,10... | collective-permute-start | bytes 589832 | tf_op jit(solution)/shard_map/ppermute | solution.py:31
  18.9 4.2 %collective-permute-start.4 = (bf16[256,768]{1,0:T(8,128)(2,1)S(1)}, bf16[256,768]{1,0:T(8,128)(2,1)S(1)}, u32[]{:S(2)}, u32[]{:S(2)}) collective-permute-start(bf16[256,768]{1,0:T(8,128)(2,1)S(1)} %pad_maximum_fusion.7), channel_id=1, source_target_pairs={{0,1},{1,0},{2,3},{3,2},{4,5},{5,4},{6,7},{7,6},{8,9},{9,8},{10,11... | collective-permute-start | bytes 1179656 | tf_op jit(solution)/shard_map/ppermute | solution.py:31
  19.3 13.5 %collective-permute-start.2 = (bf16[256,768]{1,0:T(8,128)(2,1)S(1)}, bf16[256,768]{1,0:T(8,128)(2,1)S(1)}, u32[]{:S(2)}, u32[]{:S(2)}) collective-permute-start(bf16[256,768]{1,0:T(8,128)(2,1)S(1)} %pad_maximum_fusion.7), channel_id=1, source_target_pairs={{0,4},{1,5},{2,6},{3,7},{4,8},{5,9},{6,10},{7,11},{8,12},{9,13},{1... | collective-permute-start | bytes 1179656 | tf_op jit(solution)/shard_map/ppermute | solution.py:31
  19.4 13.7 %collective-permute-start.3 = (bf16[256,768]{1,0:T(8,128)(2,1)S(1)}, bf16[256,768]{1,0:T(8,128)(2,1)S(1)}, u32[]{:S(2)}, u32[]{:S(2)}) collective-permute-start(bf16[256,768]{1,0:T(8,128)(2,1)S(1)} %pad_maximum_fusion.7), channel_id=1, source_target_pairs={{0,240},{1,241},{2,242},{3,243},{4,0},{5,1},{6,2},{7,3},{8,4},{9,5... | collective-permute-start | bytes 1179656 | tf_op jit(solution)/shard_map/ppermute | solution.py:31
  23.4 12.4 %copy-start.13 = (bf16[1536,768]{1,0:T(8,128)(2,1)S(1)}, bf16[1536,768]{1,0:T(8,128)(2,1)}, u32[]{:S(2)}) copy-start(bf16[1536,768]{1,0:T(8,128)(2,1)} %pad_maximum_fusion) | copy-start | bytes 7077892
  33.1 10.7 %collective-permute-start.6 = (bf16[256,768]{1,0:T(8,128)(2,1)S(1)}, bf16[256,768]{1,0:T(8,128)(2,1)S(1)}, u32[]{:S(2)}, u32[]{:S(2)}) collective-permute-start(bf16[256,768]{1,0:T(8,128)(2,1)S(1)} %collective-permute-done.2), channel_id=1, source_target_pairs={{0,4},{1,5},{2,6},{3,7},{4,8},{5,9},{6,10},{7,11},{8,12},{9,13},{1... | collective-permute-start | bytes 1179656 | tf_op jit(solution)/shard_map/ppermute | solution.py:31
  33.3 3.2 %collective-permute-start.8 = (bf16[256,768]{1,0:T(8,128)(2,1)S(1)}, bf16[256,768]{1,0:T(8,128)(2,1)S(1)}, u32[]{:S(2)}, u32[]{:S(2)}) collective-permute-start(bf16[256,768]{1,0:T(8,128)(2,1)S(1)} %collective-permute-done.2), channel_id=1, source_target_pairs={{0,1},{1,0},{2,3},{3,2},{4,5},{5,4},{6,7},{7,6},{8,9},{9,8},{10,11... | collective-permute-start | bytes 1179656 | tf_op jit(solution)/shard_map/ppermute | solution.py:31
  33.3 3.5 %collective-permute-start.9 = (bf16[256,768]{1,0:T(8,128)(2,1)S(1)}, bf16[256,768]{1,0:T(8,128)(2,1)S(1)}, u32[]{:S(2)}, u32[]{:S(2)}) collective-permute-start(bf16[256,768]{1,0:T(8,128)(2,1)S(1)} %collective-permute-done.3), channel_id=1, source_target_pairs={{0,1},{1,0},{2,3},{3,2},{4,5},{5,4},{6,7},{7,6},{8,9},{9,8},{10,11... | collective-permute-start | bytes 1179656 | tf_op jit(solution)/shard_map/ppermute | solution.py:31
  33.8 13.1 %collective-permute-start.10 = (bf16[256,768]{1,0:T(8,128)(2,1)S(1)}, bf16[256,768]{1,0:T(8,128)(2,1)S(1)}, u32[]{:S(2)}, u32[]{:S(2)}) collective-permute-start(bf16[256,768]{1,0:T(8,128)(2,1)S(1)} %collective-permute-done.3), channel_id=1, source_target_pairs={{0,240},{1,241},{2,242},{3,243},{4,0},{5,1},{6,2},{7,3},{8,4},{9,5... | collective-permute-start | bytes 1179656 | tf_op jit(solution)/shard_map/ppermute | solution.py:31
  43.8 3.9 %collective-permute-start.7 = (bf16[256,768]{1,0:T(8,128)(2,1)S(1)}, bf16[256,768]{1,0:T(8,128)(2,1)S(1)}, u32[]{:S(2)}, u32[]{:S(2)}) collective-permute-start(bf16[256,768]{1,0:T(8,128)(2,1)S(1)} %collective-permute-done.6), channel_id=1, source_target_pairs={{0,1},{1,0},{2,3},{3,2},{4,5},{5,4},{6,7},{7,6},{8,9},{9,8},{10,11... | collective-permute-start | bytes 1179656 | tf_op jit(solution)/shard_map/ppermute | solution.py:31
  46.9 1.8 %collective-permute-start.11 = (bf16[256,768]{1,0:T(8,128)(2,1)S(1)}, bf16[256,768]{1,0:T(8,128)(2,1)S(1)}, u32[]{:S(2)}, u32[]{:S(2)}) collective-permute-start(bf16[256,768]{1,0:T(8,128)(2,1)S(1)} %collective-permute-done.10), channel_id=1, source_target_pairs={{0,1},{1,0},{2,3},{3,2},{4,5},{5,4},{6,7},{7,6},{8,9},{9,8},{10,11... | collective-permute-start | bytes 1179656 | tf_op jit(solution)/shard_map/ppermute | solution.py:31
  56.0 10.3 %copy-start.7 = (f32[256,768]{1,0:T(8,128)}, f32[256,768]{1,0:T(8,128)S(1)}, u32[]{:S(2)}) copy-start(f32[256,768]{1,0:T(8,128)S(1)} %get-tuple-element.42.own_ref) | copy-start | bytes 2359300
  56.0 10.3 %copy-start.9 = (bf16[256,384]{1,0:T(8,128)(2,1)}, bf16[256,384]{1,0:T(8,128)(2,1)S(1)}, u32[]{:S(2)}) copy-start(bf16[256,384]{1,0:T(8,128)(2,1)S(1)} %get-tuple-element.41.dq_ref) | copy-start | bytes 589828
  56.0 10.3 %copy-start.11 = (bf16[256,384]{1,0:T(8,128)(2,1)}, bf16[256,384]{1,0:T(8,128)(2,1)S(1)}, u32[]{:S(2)}) copy-start(bf16[256,384]{1,0:T(8,128)(2,1)S(1)} %get-tuple-element.40) | copy-start | bytes 589828
  56.1 13.7 %collective-permute-start.14 = (bf16[256,768]{1,0:T(8,128)(2,1)S(1)}, bf16[256,768]{1,0:T(8,128)(2,1)S(1)}, u32[]{:S(2)}, u32[]{:S(2)}) collective-permute-start(bf16[256,768]{1,0:T(8,128)(2,1)S(1)} %get-tuple-element.43.refs_5_), channel_id=1, source_target_pairs={{0,240},{1,241},{2,242},{3,243},{4,0},{5,1},{6,2},{7,3},{8,4},{9,5... | collective-permute-start | bytes 1179656 | tf_op jit(solution)/shard_map/ppermute | solution.py:31
  56.1 14.5 %collective-permute-start.16 = (bf16[256,768]{1,0:T(8,128)(2,1)S(1)}, bf16[256,768]{1,0:T(8,128)(2,1)S(1)}, u32[]{:S(2)}, u32[]{:S(2)}) collective-permute-start(bf16[256,768]{1,0:T(8,128)(2,1)S(1)} %get-tuple-element.47.refs_9_), channel_id=1, source_target_pairs={{0,4},{1,5},{2,6},{3,7},{4,8},{5,9},{6,10},{7,11},{8,12},{9,13},{1... | collective-permute-start | bytes 1179656 | tf_op jit(solution)/shard_map/ppermute | solution.py:31
  66.4 14.9 %copy-start.1 = (bf16[2,4,48,1152]{3,2,1,0:T(8,128)(2,1)S(1)}, bf16[2,4,48,1152]{3,2,1,0:T(8,128)(2,1)}, u32[]{:S(2)}) copy-start(bf16[2,4,48,1152]{3,2,1,0:T(8,128)(2,1)} %get-tuple-element.48.refs_0_) | copy-start | bytes 2654212
  66.4 14.9 %copy-start.2 = (bf16[2,4,48,1152]{3,2,1,0:T(8,128)(2,1)S(1)}, bf16[2,4,48,1152]{3,2,1,0:T(8,128)(2,1)}, u32[]{:S(2)}) copy-start(bf16[2,4,48,1152]{3,2,1,0:T(8,128)(2,1)} %get-tuple-element.49.refs_1_) | copy-start | bytes 2654212
  66.4 13.3 %collective-permute-start.12 = (bf16[2,4,48,1152]{3,2,1,0:T(8,128)(2,1)}, bf16[2,4,48,1152]{3,2,1,0:T(8,128)(2,1)S(1)}, u32[]{:S(2)}, u32[]{:S(2)}) collective-permute-start(bf16[2,4,48,1152]{3,2,1,0:T(8,128)(2,1)} %get-tuple-element.50), channel_id=1, source_target_pairs={{0,64},{1,193},{2,66},{3,195},{4,68},{5,197},{6,70},{7,199},{8,72}... | collective-permute-start | bytes 2654216 | tf_op jit(solution)/shard_map/ppermute | solution.py:31
  68.0 13.3 %collective-permute-start.13 = (bf16[2,4,48,1152]{3,2,1,0:T(8,128)(2,1)}, bf16[2,4,48,1152]{3,2,1,0:T(8,128)(2,1)S(1)}, u32[]{:S(2)}, u32[]{:S(2)}) collective-permute-start(bf16[2,4,48,1152]{3,2,1,0:T(8,128)(2,1)} %get-tuple-element.51), channel_id=1, source_target_pairs={{0,16},{1,49},{2,18},{3,51},{4,20},{5,53},{6,22},{7,55},{8,24},{9,... | collective-permute-start | bytes 2654216 | tf_op jit(solution)/shard_map/ppermute | solution.py:31
  70.6 22.0 %collective-permute-start.15 = (bf16[256,768]{1,0:T(8,128)(2,1)}, bf16[256,768]{1,0:T(8,128)(2,1)}, u32[]{:S(2)}, u32[]{:S(2)}) collective-permute-start(bf16[256,768]{1,0:T(8,128)(2,1)} %add_convert_fusion.2), channel_id=1, source_target_pairs={{0,240},{1,241},{2,242},{3,243},{4,0},{5,1},{6,2},{7,3},{8,4},{9,5... | collective-permute-start | bytes 1179656 | tf_op jit(solution)/shard_map/ppermute | solution.py:31
  71.5 21.1 %collective-permute-start.17 = (bf16[256,768]{1,0:T(8,128)(2,1)}, bf16[256,768]{1,0:T(8,128)(2,1)}, u32[]{:S(2)}, u32[]{:S(2)}) collective-permute-start(bf16[256,768]{1,0:T(8,128)(2,1)} %add_convert_fusion.1), channel_id=1, source_target_pairs={{0,4},{1,5},{2,6},{3,7},{4,8},{5,9},{6,10},{7,11},{8,12},{9,13},{1... | collective-permute-start | bytes 1179656 | tf_op jit(solution)/shard_map/ppermute | solution.py:31
  81.2 11.4 %copy-start.8 = (f32[256,768]{1,0:T(8,128)S(1)}, f32[256,768]{1,0:T(8,128)}, u32[]{:S(2)}) copy-start(f32[256,768]{1,0:T(8,128)} %copy-done.7) | copy-start | bytes 2359300
  81.2 11.4 %copy-start.10 = (bf16[256,384]{1,0:T(8,128)(2,1)S(1)}, bf16[256,384]{1,0:T(8,128)(2,1)}, u32[]{:S(2)}) copy-start(bf16[256,384]{1,0:T(8,128)(2,1)} %copy-done.9) | copy-start | bytes 589828
  82.5 0.9 copy-start.5
  83.4 13.3 %copy-start.3 = (f32[4,48,1152]{2,1,0:T(8,128)}, f32[4,48,1152]{2,1,0:T(8,128)S(1)}, u32[]{:S(2)}) copy-start(f32[4,48,1152]{2,1,0:T(8,128)S(1)} %get-tuple-element.57.refs_0_) | copy-start | bytes 2654212
  83.4 17.8 %collective-permute-start.20 = (bf16[4,48,1152]{2,1,0:T(8,128)(2,1)}, bf16[4,48,1152]{2,1,0:T(8,128)(2,1)S(1)}, u32[]{:S(2)}, u32[]{:S(2)}) collective-permute-start(bf16[4,48,1152]{2,1,0:T(8,128)(2,1)} %get-tuple-element.52), channel_id=1, source_target_pairs={{0,192},{1,65},{2,194},{3,67},{4,196},{5,69},{6,198},{7,71},{8,200... | collective-permute-start | bytes 1327112 | tf_op jit(solution)/shard_map/ppermute | solution.py:31
  92.5 9.7 %collective-permute-start.21 = (bf16[4,48,1152]{2,1,0:T(8,128)(2,1)}, bf16[4,48,1152]{2,1,0:T(8,128)(2,1)S(1)}, u32[]{:S(2)}, u32[]{:S(2)}) collective-permute-start(bf16[4,48,1152]{2,1,0:T(8,128)(2,1)} %get-tuple-element.59), channel_id=1, source_target_pairs={{0,48},{1,17},{2,50},{3,19},{4,52},{5,21},{6,54},{7,23},{8,56},{9,... | collective-permute-start | bytes 1327112 | tf_op jit(solution)/shard_map/ppermute | solution.py:31
  92.6 9.6 %copy-start.6 = (f32[4,48,1152]{2,1,0:T(8,128)S(1)}, f32[4,48,1152]{2,1,0:T(8,128)}, u32[]{:S(2)}) copy-start(f32[4,48,1152]{2,1,0:T(8,128)} %copy-done.5) | copy-start | bytes 2654212
  96.7 8.1 %collective-permute-start.18 = (bf16[2,256,384]{2,1,0:T(8,128)(2,1)S(1)}, bf16[2,256,384]{2,1,0:T(8,128)(2,1)}, u32[]{:S(2)}, u32[]{:S(2)}) collective-permute-start(bf16[2,256,384]{2,1,0:T(8,128)(2,1)S(1)} %get-tuple-element.56), channel_id=1, source_target_pairs={{0,1},{1,0},{2,3},{3,2},{4,5},{5,4},{6,7},{7,6},{8,9},{9,8},{10,11... | collective-permute-start | bytes 1179656 | tf_op jit(solution)/shard_map/ppermute | solution.py:31
  102.2 1.2 copy-start.4
  104.1 6.0 %collective-permute-start.22 = (bf16[2,48,1152]{2,1,0:T(8,128)(2,1)S(1)}, bf16[2,48,1152]{2,1,0:T(8,128)(2,1)S(1)}, u32[]{:S(2)}, u32[]{:S(2)}) collective-permute-start(bf16[2,48,1152]{2,1,0:T(8,128)(2,1)S(1)} %get-tuple-element.61), channel_id=1, source_target_pairs={{0,16},{1,49},{2,18},{3,51},{4,20},{5,53},{6,22},{7,55},{8,24},{9,... | collective-permute-start | bytes 663560 | tf_op jit(solution)/shard_map/ppermute | solution.py:31
  104.7 10.0 %copy-start.12 = (bf16[256,384]{1,0:T(8,128)(2,1)S(1)}, bf16[256,384]{1,0:T(8,128)(2,1)}, u32[]{:S(2)}) copy-start(bf16[256,384]{1,0:T(8,128)(2,1)} %copy-done.11) | copy-start | bytes 589828
  105.9 8.7 %collective-permute-start.24 = (bf16[256,384]{1,0:T(8,128)(2,1)S(1)}, bf16[256,384]{1,0:T(8,128)(2,1)S(1)}, u32[]{:S(2)}, u32[]{:S(2)}) collective-permute-start(bf16[256,384]{1,0:T(8,128)(2,1)S(1)} %get-tuple-element.82), channel_id=1, source_target_pairs={{0,2},{1,3},{2,0},{3,1},{4,6},{5,7},{6,4},{7,5},{8,10},{9,11},{10,... | collective-permute-start | bytes 589832 | tf_op jit(solution)/shard_map/ppermute | solution.py:31
  106.0 6.0 %collective-permute-start.23 = (bf16[2,48,1152]{2,1,0:T(8,128)(2,1)S(1)}, bf16[2,48,1152]{2,1,0:T(8,128)(2,1)S(1)}, u32[]{:S(2)}, u32[]{:S(2)}) collective-permute-start(bf16[2,48,1152]{2,1,0:T(8,128)(2,1)S(1)} %get-tuple-element.63), channel_id=1, source_target_pairs={{0,64},{1,193},{2,66},{3,195},{4,68},{5,197},{6,70},{7,199},{8,72}... | collective-permute-start | bytes 663560 | tf_op jit(solution)/shard_map/ppermute | solution.py:31
  114.7 6.0 %collective-permute-start.26 = (bf16[48,1152]{1,0:T(8,128)(2,1)S(1)}, bf16[48,1152]{1,0:T(8,128)(2,1)S(1)}, u32[]{:S(2)}, u32[]{:S(2)}) collective-permute-start(bf16[48,1152]{1,0:T(8,128)(2,1)S(1)} %fusion.8), channel_id=1, source_target_pairs={{0,192},{1,65},{2,194},{3,67},{4,196},{5,69},{6,198},{7,71},{8,200... | collective-permute-start | bytes 331784 | tf_op jit(solution)/shard_map/ppermute | solution.py:31
  114.8 15.4 %collective-permute-start.19 = (bf16[2,256,384]{2,1,0:T(8,128)(2,1)S(1)}, bf16[2,256,384]{2,1,0:T(8,128)(2,1)S(1)}, u32[]{:S(2)}, u32[]{:S(2)}) collective-permute-start(bf16[2,256,384]{2,1,0:T(8,128)(2,1)S(1)} %pad_maximum_fusion.8), channel_id=1, source_target_pairs={{0,0},{1,1},{2,2},{3,3},{4,4},{5,5},{6,6},{7,7},{8,8},{9,9},{10,10... | collective-permute-start | bytes 1179656 | tf_op jit(solution)/shard_map/ppermute | solution.py:31
  119.7 6.0 %collective-permute-start.25 = (bf16[48,1152]{1,0:T(8,128)(2,1)S(1)}, bf16[48,1152]{1,0:T(8,128)(2,1)S(1)}, u32[]{:S(2)}, u32[]{:S(2)}) collective-permute-start(bf16[48,1152]{1,0:T(8,128)(2,1)S(1)} %fusion.7), channel_id=1, source_target_pairs={{0,48},{1,17},{2,50},{3,19},{4,52},{5,21},{6,54},{7,23},{8,56},{9,... | collective-permute-start | bytes 331784 | tf_op jit(solution)/shard_map/ppermute | solution.py:31
  125.9 6.6 %collective-permute-start.29 = (bf16[24,1152]{1,0:T(8,128)(2,1)S(1)}, bf16[24,1152]{1,0:T(8,128)(2,1)S(1)}, u32[]{:S(2)}, u32[]{:S(2)}) collective-permute-start(bf16[24,1152]{1,0:T(8,128)(2,1)S(1)} %get-tuple-element.80), channel_id=1, source_target_pairs={{0,12},{1,13},{2,14},{3,15},{4,0},{5,1},{6,2},{7,3},{8,4},{9,5},{1... | collective-permute-start | bytes 165896 | tf_op jit(solution)/shard_map/ppermute | solution.py:31
  126.8 7.9 %collective-permute-start.28 = (bf16[24,1152]{1,0:T(8,128)(2,1)S(1)}, bf16[24,1152]{1,0:T(8,128)(2,1)S(1)}, u32[]{:S(2)}, u32[]{:S(2)}) collective-permute-start(bf16[24,1152]{1,0:T(8,128)(2,1)S(1)} %get-tuple-element.81), channel_id=1, source_target_pairs={{0,8},{1,9},{2,10},{3,11},{4,12},{5,13},{6,14},{7,15},{8,0},{9,1},... | collective-permute-start | bytes 165896 | tf_op jit(solution)/shard_map/ppermute | solution.py:31
  126.8 7.9 %collective-permute-start.27 = (bf16[24,1152]{1,0:T(8,128)(2,1)S(1)}, bf16[24,1152]{1,0:T(8,128)(2,1)S(1)}, u32[]{:S(2)}, u32[]{:S(2)}) collective-permute-start(bf16[24,1152]{1,0:T(8,128)(2,1)S(1)} %get-tuple-element.79), channel_id=1, source_target_pairs={{0,4},{1,5},{2,6},{3,7},{4,8},{5,9},{6,10},{7,11},{8,12},{9,13},{1... | collective-permute-start | bytes 165896 | tf_op jit(solution)/shard_map/ppermute | solution.py:31

commit v3 on v2

--- a/solution.py
+++ b/solution.py
@@ -182,8 +182,9 @@
 
 
 def first_sums_kernel(*refs):
-    kept, got, sent, mine = refs[:2], refs[2:4], refs[4:6], refs[6:]
-    for n in range(2):
+    count = len(refs) // 4
+    kept, got, sent, mine = (refs[i * count : (i + 1) * count] for i in range(4))
+    for n in range(count):
         sent[n][...] = (kept[n][1].astype(F32) + got[n][1].astype(F32)).astype(BF16)
         mine[n][...] = kept[n][0].astype(F32) + got[n][0].astype(F32)
 
@@ -193,8 +194,8 @@
         first_sums_kernel,
         out_shape=[jax.ShapeDtypeStruct(k.shape[1:], BF16) for k in kept]
         + [jax.ShapeDtypeStruct(k.shape[1:], F32) for k in kept],
-        in_specs=[VMEM] * 4,
-        out_specs=[VMEM] * 4,
+        in_specs=[VMEM] * (2 * len(kept)),
+        out_specs=[VMEM] * (2 * len(kept)),
         compiler_params=ROOMY,
     )(*kept, *got)
 
@@ -349,7 +350,9 @@
     ).astype(jnp.int32)
     sent_x, kept_x, sent_y, kept_y = weight_terms(order, grad_query, tokens, grads)
     got = [move(sent_x, partner(0, firstly)), move(sent_y, partner(1, firstly))]
-    pass_x, pass_y, *sums = first_sums((kept_x, kept_y), got)
+    pass_x, sum_x = first_sums((kept_x,), got[:1])
+    pass_y, sum_y = first_sums((kept_y,), got[1:])
+    sums = [sum_x, sum_y]
     pass_one = pass_x
     got = [move(pass_x, partner(0, secondly)), move(pass_y, partner(1, secondly))]
     sent_x, sent_y, kept_x, kept_y = second_sums(order, sums, got)

time: 136 us -> 135 us (level)
  starting transfers between devices: 53.3 us -> 50.7 us
    ppermute x30, starting transfers between devices: 53.3 us -> 50.7 us  [move(): lax.ppermute(value, AXES, [(i, flat(*to(*coords(i)))) for i in range(256)])]
  transfers between devices with their start and end apart: 30 -> 30, of which waited for: 17 -> 15; matrix products, arithmetic and copies ran while one was open for 12% -> 12% of each run, Pallas kernels for 9% -> 10%
where the time goes in v3:
time: 135 us; the launch traced here: 134 us
  starting transfers between devices  50.7 us (38%)
  waiting for transfers between devices  44.4 us (33%)
  Pallas kernels  19.3 us (14%)
  other arithmetic  7.23 us (5%)
  matrix products  5.89 us (4%)
  local copies, waits for them, and re-layouts  5.54 us (4%)
    ppermute x30, starting transfers between devices, move(): lax.ppermute(value, AXES, [(i, flat(*to(*coords(i)))) for i in range(256)])  50.7 us
    ppermute x30, waiting for transfers between devices, move(): lax.ppermute(value, AXES, [(i, flat(*to(*coords(i)))) for i in range(256)])  44.4 us
    pallas_call x1, Pallas kernels, attention(): pl.pallas_call(attention_kernel, out_shape=[jax.ShapeDtypeStruct((rows, w...  6.21 us
    pallas_call x1, Pallas kernels, weight_terms(): pl.pallas_call(weight_kernel, out_shape=[jax.ShapeDtypeStruct(shape, BF16...  6.17 us
    dot_general x6, matrix products, dot(): return lax.dot_general(a, b, dims, preferred_element_type=F32)  5.89 us
    pallas_call x1, Pallas kernels, input_terms(): pl.pallas_call(input_kernel, out_shape=[jax.ShapeDtypeStruct((2, rows, wi...  3.9 us
  transfers between devices with their start and end apart: 30, of which 15 were waited for; matrix products, arithmetic and copies ran while one was open for 12% of the time, Pallas kernels for 10%

profile of v3, /device:TPU:24, one launch (start us, length us, event | category | flops | bytes accessed | tf_op | source)
XLA Modules:
  0.0 134.5 jit_solution(7063810403734122005)
XLA Ops:
  0.6 6.5 %collective-permute-start = (bf16[256,384]{1,0:T(8,128)(2,1)}, bf16[256,384]{1,0:T(8,128)(2,1)S(1)}, u32[]{:S(2)}, u32[]{:S(2)}) collective-permute-start(bf16[256,384]{1,0:T(8,128)(2,1)} %param.4), channel_id=1, source_target_pairs={{0,0},{1,1},{2,2},{3,3},{4,4},{5,5},{6,6},{7,7},{8,8},{9,9},{10,10... | collective-permute-start | bytes 589832 | tf_op jit(solution)/shard_map/ppermute | solution.py:31
  7.2 3.2 %collective-permute-start.1 = (bf16[256,384]{1,0:T(8,128)(2,1)}, bf16[256,384]{1,0:T(8,128)(2,1)S(1)}, u32[]{:S(2)}, u32[]{:S(2)}) collective-permute-start(bf16[256,384]{1,0:T(8,128)(2,1)} %param.4), channel_id=1, source_target_pairs={{0,2},{1,3},{2,0},{3,1},{4,6},{5,7},{6,4},{7,5},{8,10},{9,11},{10,... | collective-permute-start | bytes 589832 | tf_op jit(solution)/shard_map/ppermute | solution.py:31
  10.4 3.8 %collective-permute-start.5 = (bf16[256,384]{1,0:T(8,128)(2,1)}, bf16[256,384]{1,0:T(8,128)(2,1)S(1)}, u32[]{:S(2)}, u32[]{:S(2)}) collective-permute-start(bf16[256,384]{1,0:T(8,128)(2,1)} %param.6), channel_id=1, source_target_pairs={{0,0},{1,1},{2,2},{3,3},{4,4},{5,5},{6,6},{7,7},{8,8},{9,9},{10,10... | collective-permute-start | bytes 589832 | tf_op jit(solution)/shard_map/ppermute | solution.py:31
  14.3 1.9 %slice_bitcast_fusion.1 = (bf16[1536,384]{1,0:T(8,128)(2,1)S(1)}, bf16[1536,384]{1,0:T(8,128)(2,1)S(1)}) fusion(bf16[3,1536,384]{2,1,0:T(8,128)(2,1)} %weight_ref.1), kind=kLoop, calls=%fused_computation.10 | loop fusion | bytes 4718592 | tf_op jit(solution)/shard_map/squeeze | solution.py:309
  16.3 0.1 copy.8
  16.4 1.6 %pad_maximum_fusion = bf16[1536,768]{1,0:T(8,128)(2,1)} fusion(bf16[1536,384]{1,0:T(8,128)(2,1)S(1)} %get-tuple-element.68, bf16[1536,384]{1,0:T(8,128)(2,1)S(1)} %get-tuple-element.67), kind=kLoop, calls=%fused_computation | loop fusion | flops 4718592 | bytes 4718592 | tf_op jit(solution)/shard_map/concatenate | solution.py:309
  18.0 0.2 compare_reduce_fusion
  18.2 0.6 collective-permute-done.1
  18.9 0.1 collective-permute-start.4
  19.0 0.1 copy.9
  19.4 3.7 %collective-permute-start.3 = (bf16[256,768]{1,0:T(8,128)(2,1)S(1)}, bf16[256,768]{1,0:T(8,128)(2,1)S(1)}, u32[]{:S(2)}, u32[]{:S(2)}) collective-permute-start(bf16[256,768]{1,0:T(8,128)(2,1)S(1)} %pad_maximum_fusion.7), channel_id=1, source_target_pairs={{0,240},{1,241},{2,242},{3,243},{4,0},{5,1},{6,2},{7,3},{8,4},{9,5... | collective-permute-start | bytes 1179656 | tf_op jit(solution)/shard_map/ppermute | solution.py:31
  23.1 0.1 broadcast_select_fusion.9
  23.4 2.0 %fusion.3.q_ref = bf16[256,384]{1,0:T(8,128)(2,1)S(1)} fusion(bf16[3,1536,384]{2,1,0:T(8,128)(2,1)} %weight_ref.1, bf16[256,384]{1,0:T(8,128)(2,1)S(1)} %get-tuple-element.111, bf16[256,384]{1,0:T(8,128)(2,1)S(1)} %get-tuple-element.101, bf16[256,384]{1,0:T(8,128)(2,1)S(1)} %get-tuple-element.112, bf16[256,384]{1,0:T(8,128)(2,1)S(1)} %get-tuple-element.100), kind=kOutput, calls=%fused_computation.11 | convolution fusion | flops 305233920 | bytes 2162688 | tf_op jit(solution)/shard_map/dot_general | solution.py:64
  25.4 7.4 %collective-permute-done.2 = bf16[256,768]{1,0:T(8,128)(2,1)S(1)} collective-permute-done((bf16[256,768]{1,0:T(8,128)(2,1)S(1)}, bf16[256,768]{1,0:T(8,128)(2,1)S(1)}, u32[]{:S(2)}, u32[]{:S(2)}) %collective-permute-start.2) | collective-permute-done | bytes 393248 | tf_op jit(solution)/shard_map/ppermute | solution.py:31
  32.8 0.3 collective-permute-done.3
  33.1 0.2 collective-permute-start.6
  33.3 0.5 collective-permute-start.9
  33.8 1.8 %collective-permute-start.10 = (bf16[256,768]{1,0:T(8,128)(2,1)S(1)}, bf16[256,768]{1,0:T(8,128)(2,1)S(1)}, u32[]{:S(2)}, u32[]{:S(2)}) collective-permute-start(bf16[256,768]{1,0:T(8,128)(2,1)S(1)} %collective-permute-done.3), channel_id=1, source_target_pairs={{0,240},{1,241},{2,242},{3,243},{4,0},{5,1},{6,2},{7,3},{8,4},{9,5... | collective-permute-start | bytes 1179656 | tf_op jit(solution)/shard_map/ppermute | solution.py:31
  35.7 0.8 convolution_convert_fusion.2.refs_2_
  36.9 0.8 convolution_convert_fusion.3.refs_1_
  37.7 6.2 %collective-permute-done.6 = bf16[256,768]{1,0:T(8,128)(2,1)S(1)} collective-permute-done((bf16[256,768]{1,0:T(8,128)(2,1)S(1)}, bf16[256,768]{1,0:T(8,128)(2,1)S(1)}, u32[]{:S(2)}, u32[]{:S(2)}) %collective-permute-start.6) | collective-permute-done | bytes 393248 | tf_op jit(solution)/shard_map/ppermute | solution.py:31
  44.0 3.0 %collective-permute-done.10 = bf16[256,768]{1,0:T(8,128)(2,1)S(1)} collective-permute-done((bf16[256,768]{1,0:T(8,128)(2,1)S(1)}, bf16[256,768]{1,0:T(8,128)(2,1)S(1)}, u32[]{:S(2)}, u32[]{:S(2)}) %collective-permute-start.10) | collective-permute-done | bytes 393248 | tf_op jit(solution)/shard_map/ppermute | solution.py:31
  46.9 0.8 convolution_convert_fusion.1.refs_3_
  48.0 0.8 convolution_convert_fusion.4.refs_0_
  48.9 0.8 convolution_convert_fusion.refs_4_
  49.8 6.2 %shard_map.67 = (bf16[256,384]{1,0:T(8,128)(2,1)S(1)}, bf16[256,384]{1,0:T(8,128)(2,1)S(1)}, f32[256,768]{1,0:T(8,128)S(1)}, bf16[256,768]{1,0:T(8,128)(2,1)S(1)...) custom-call(bf16[256,384]{1,0:T(8,128)(2,1)S(1)} %fusion.3.q_ref, ...), custom_call_target="tpu_custom_call" | custom-call | flops 1509949440 | bytes 3932160 | tf_op jit(solution)/shard_map/pallas_call | solution.py:115
  56.1 0.1 collective-permute-start.13
  56.1 4.1 %collective-permute-start.15 = (bf16[256,768]{1,0:T(8,128)(2,1)S(1)}, bf16[256,768]{1,0:T(8,128)(2,1)S(1)}, u32[]{:S(2)}, u32[]{:S(2)}) collective-permute-start(bf16[256,768]{1,0:T(8,128)(2,1)S(1)} %get-tuple-element.47.refs_9_), channel_id=1, source_target_pairs={{0,4},{1,5},{2,6},{3,7},{4,8},{5,9},{6,10},{7,11},{8,12},{9,13},{1... | collective-permute-start | bytes 1179656 | tf_op jit(solution)/shard_map/ppermute | solution.py:31
  60.3 6.2 %shard_map.68 = (bf16[2,4,48,1152]{3,2,1,0:T(8,128)(2,1)}, bf16[2,4,48,1152]{3,2,1,0:T(8,128)(2,1)}, bf16[2,4,48,1152]{3,2,1,0:T(8,128)(2,1)}, bf16[2,4,48,1152]{3,2,1,0:T(8,128)(2,1)}) custom-call(s32[2,4]{1,0:T(2,128)S(1)} %pad_add_fusion.order_ref, bf16[256,384]{1,0:T(8,128)(2,1)S(1)} %get-tuple-element.41.dq_ref, ...), custom_call_target="tpu_custom_call" | custom-call | flops 3300000000 | bytes 30000000 | tf_op jit(solution)/shard_map/pallas_call | solution.py:171
  66.5 1.6 %collective-permute-start.12 = (bf16[2,4,48,1152]{3,2,1,0:T(8,128)(2,1)}, bf16[2,4,48,1152]{3,2,1,0:T(8,128)(2,1)S(1)}, u32[]{:S(2)}, u32[]{:S(2)}) collective-permute-start(bf16[2,4,48,1152]{3,2,1,0:T(8,128)(2,1)} %get-tuple-element.49), channel_id=1, source_target_pairs={{0,64},{1,193},{2,66},{3,195},{4,68},{5,197},{6,70},{7,199},{8,72}... | collective-permute-start | bytes 2654216 | tf_op jit(solution)/shard_map/ppermute | solution.py:31
  68.0 1.7 %collective-permute-done.13 = bf16[256,768]{1,0:T(8,128)(2,1)S(1)} collective-permute-done((bf16[256,768]{1,0:T(8,128)(2,1)S(1)}, bf16[256,768]{1,0:T(8,128)(2,1)S(1)}, u32[]{:S(2)}, u32[]{:S(2)}) %collective-permute-start.13) | collective-permute-done | bytes 393248 | tf_op jit(solution)/shard_map/ppermute | solution.py:31
  69.8 0.9 add_convert_fusion.2
  70.6 0.9 add_convert_fusion.1
  71.5 4.1 %collective-permute-start.16 = (bf16[256,768]{1,0:T(8,128)(2,1)}, bf16[256,768]{1,0:T(8,128)(2,1)}, u32[]{:S(2)}, u32[]{:S(2)}) collective-permute-start(bf16[256,768]{1,0:T(8,128)(2,1)} %add_convert_fusion.1), channel_id=1, source_target_pairs={{0,4},{1,5},{2,6},{3,7},{4,8},{5,9},{6,10},{7,11},{8,12},{9,13},{1... | collective-permute-start | bytes 1179656 | tf_op jit(solution)/shard_map/ppermute | solution.py:31
  75.6 4.2 %collective-permute-done.12.refs_1_ = bf16[2,4,48,1152]{3,2,1,0:T(8,128)(2,1)S(1)} collective-permute-done((bf16[2,4,48,1152]{3,2,1,0:T(8,128)(2,1)}, bf16[2,4,48,1152]{3,2,1,0:T(8,128)(2,1)S(1)}, u32[]{:S(2)}, u32[]{:S(2)}) %collective-permute-start.12) | collective-permute-done | bytes 884768 | tf_op jit(solution)/shard_map/ppermute | solution.py:31
  79.8 0.9 copy-done.3
  80.7 1.2 copy-done.4
  81.9 0.9 shard_map.69
  82.8 10.6 %collective-permute-start.20 = (bf16[4,48,1152]{2,1,0:T(8,128)(2,1)}, bf16[4,48,1152]{2,1,0:T(8,128)(2,1)}, u32[]{:S(2)}, u32[]{:S(2)}) collective-permute-start(bf16[4,48,1152]{2,1,0:T(8,128)(2,1)} %get-tuple-element.50), channel_id=1, source_target_pairs={{0,192},{1,65},{2,194},{3,67},{4,196},{5,69},{6,198},{7,71},{8,200... | collective-permute-start | bytes 1327112 | tf_op jit(solution)/shard_map/ppermute | solution.py:31
  93.4 0.9 shard_map.71
  94.4 3.9 %shard_map.70 = (bf16[2,256,384]{2,1,0:T(8,128)(2,1)S(1)}, f32[2,256,384]{2,1,0:T(8,128)S(1)}) custom-call(s32[4]{0:T(128)S(1)} %pad_add_fusion.1.place_ref, bf16[256,384]{1,0:T(8,128)(2,1)S(1)} %copy-done.8, f32[256,768]{1,0:T(8,128)S(1)} %copy-done.6, bf16[3,1536,384]{2,1,0:T(8,128)(2,1)} %weight_ref.1, bf16[256,768]{1,0:T(8,128)(2,1)} %collective-permute-done.14.refs_0_, ...), custom_call_target="tpu_custom_call" | custom-call | tf_op jit(solution)/shard_map/pallas_call | solution.py:247
  98.3 1.1 collective-permute-start.17
  99.4 0.6 collective-permute-done.20.refs_2_
  100.0 4.0 %collective-permute-done.21.refs_3_ = bf16[4,48,1152]{2,1,0:T(8,128)(2,1)S(1)} collective-permute-done((bf16[4,48,1152]{2,1,0:T(8,128)(2,1)}, bf16[4,48,1152]{2,1,0:T(8,128)(2,1)S(1)}, u32[]{:S(2)}, u32[]{:S(2)}) %collective-permute-start.21) | collective-permute-done | bytes 442400 | tf_op jit(solution)/shard_map/ppermute | solution.py:31
  104.0 1.2 shard_map.72
  105.2 0.1 collective-permute-start.22
  105.3 1.1 add_convert_fusion
  106.5 0.1 collective-permute-start.24
  106.6 0.1 collective-permute-start.23
  106.7 4.5 %collective-permute-done.22 = bf16[2,48,1152]{2,1,0:T(8,128)(2,1)S(1)} collective-permute-done((bf16[2,48,1152]{2,1,0:T(8,128)(2,1)S(1)}, bf16[2,48,1152]{2,1,0:T(8,128)(2,1)S(1)}, u32[]{:S(2)}, u32[]{:S(2)}) %collective-permute-start.22) | collective-permute-done | bytes 221216 | tf_op jit(solution)/shard_map/ppermute | solution.py:31
  111.3 1.4 %collective-permute-done.23 = bf16[2,48,1152]{2,1,0:T(8,128)(2,1)S(1)} collective-permute-done((bf16[2,48,1152]{2,1,0:T(8,128)(2,1)S(1)}, bf16[2,48,1152]{2,1,0:T(8,128)(2,1)S(1)}, u32[]{:S(2)}, u32[]{:S(2)}) %collective-permute-start.23) | collective-permute-done | bytes 221216 | tf_op jit(solution)/shard_map/ppermute | solution.py:31
  112.7 0.9 collective-permute-done.24
  113.5 0.9 collective-permute-start.26
  114.4 5.8 %collective-permute-start.18 = (bf16[2,256,384]{2,1,0:T(8,128)(2,1)S(1)}, bf16[2,256,384]{2,1,0:T(8,128)(2,1)S(1)}, u32[]{:S(2)}, u32[]{:S(2)}) collective-permute-start(bf16[2,256,384]{2,1,0:T(8,128)(2,1)S(1)} %pad_maximum_fusion.8), channel_id=1, source_target_pairs={{0,0},{1,1},{2,2},{3,3},{4,4},{5,5},{6,6},{7,7},{8,8},{9,9},{10,10... | collective-permute-start | bytes 1179656 | tf_op jit(solution)/shard_map/ppermute | solution.py:31
  120.3 0.1 collective-permute-start.25
  120.4 5.9 %collective-permute-done.25 = bf16[48,1152]{1,0:T(8,128)(2,1)S(1)} collective-permute-done((bf16[48,1152]{1,0:T(8,128)(2,1)S(1)}, bf16[48,1152]{1,0:T(8,128)(2,1)S(1)}, u32[]{:S(2)}, u32[]{:S(2)}) %collective-permute-start.25) | collective-permute-done | bytes 110624 | tf_op jit(solution)/shard_map/ppermute | solution.py:31
  126.4 0.1 collective-permute-start.29
  126.5 0.1 collective-permute-start.28
  126.6 1.9 %collective-permute-start.27 = (bf16[24,1152]{1,0:T(8,128)(2,1)S(1)}, bf16[24,1152]{1,0:T(8,128)(2,1)S(1)}, u32[]{:S(2)}, u32[]{:S(2)}) collective-permute-start(bf16[24,1152]{1,0:T(8,128)(2,1)S(1)} %get-tuple-element.79), channel_id=1, source_target_pairs={{0,4},{1,5},{2,6},{3,7},{4,8},{5,9},{6,10},{7,11},{8,12},{9,13},{1... | collective-permute-start | bytes 165896 | tf_op jit(solution)/shard_map/ppermute | solution.py:31
  128.5 1.5 %collective-permute-done.18 = bf16[2,256,384]{2,1,0:T(8,128)(2,1)S(1)} collective-permute-done((bf16[2,256,384]{2,1,0:T(8,128)(2,1)S(1)}, bf16[2,256,384]{2,1,0:T(8,128)(2,1)S(1)}, u32[]{:S(2)}, u32[]{:S(2)}) %collective-permute-start.18) | collective-permute-done | bytes 393248 | tf_op jit(solution)/shard_map/ppermute | solution.py:31
  130.0 0.7 fusion.6
  130.8 0.7 slice_bitcast_fusion.3
  131.5 2.3 %collective-permute-done.28 = bf16[24,1152]{1,0:T(8,128)(2,1)S(1)} collective-permute-done((bf16[24,1152]{1,0:T(8,128)(2,1)S(1)}, bf16[24,1152]{1,0:T(8,128)(2,1)S(1)}, u32[]{:S(2)}, u32[]{:S(2)}) %collective-permute-start.28) | collective-permute-done | bytes 55328 | tf_op jit(solution)/shard_map/ppermute | solution.py:31
  133.8 0.7 pad_maximum_fusion.9
  (83 shorter events, 1.9 us)
Async XLA Ops:
  0.6 15.6 %copy-start = (s32[128,9]{0,1:T(8,128)S(1)}, s32[128,9]{0,1:T(8,128)}, u32[]{:S(2)}) copy-start(s32[128,9]{0,1:T(8,128)} %param.7) | copy-start | bytes 13828
  0.6 18.2 %collective-permute-start = (bf16[256,384]{1,0:T(8,128)(2,1)}, bf16[256,384]{1,0:T(8,128)(2,1)S(1)}, u32[]{:S(2)}, u32[]{:S(2)}) collective-permute-start(bf16[256,384]{1,0:T(8,128)(2,1)} %param.4), channel_id=1, source_target_pairs={{0,0},{1,1},{2,2},{3,3},{4,4},{5,5},{6,6},{7,7},{8,8},{9,9},{10,10... | collective-permute-start | bytes 589832 | tf_op jit(solution)/shard_map/ppermute | solution.py:31
  7.2 11.6 %collective-permute-start.1 = (bf16[256,384]{1,0:T(8,128)(2,1)}, bf16[256,384]{1,0:T(8,128)(2,1)S(1)}, u32[]{:S(2)}, u32[]{:S(2)}) collective-permute-start(bf16[256,384]{1,0:T(8,128)(2,1)} %param.4), channel_id=1, source_target_pairs={{0,2},{1,3},{2,0},{3,1},{4,6},{5,7},{6,4},{7,5},{8,10},{9,11},{10,... | collective-permute-start | bytes 589832 | tf_op jit(solution)/shard_map/ppermute | solution.py:31
  10.4 39.4 %collective-permute-start.5 = (bf16[256,384]{1,0:T(8,128)(2,1)}, bf16[256,384]{1,0:T(8,128)(2,1)S(1)}, u32[]{:S(2)}, u32[]{:S(2)}) collective-permute-start(bf16[256,384]{1,0:T(8,128)(2,1)} %param.6), channel_id=1, source_target_pairs={{0,0},{1,1},{2,2},{3,3},{4,4},{5,5},{6,6},{7,7},{8,8},{9,9},{10,10... | collective-permute-start | bytes 589832 | tf_op jit(solution)/shard_map/ppermute | solution.py:31
  18.9 4.2 %collective-permute-start.4 = (bf16[256,768]{1,0:T(8,128)(2,1)S(1)}, bf16[256,768]{1,0:T(8,128)(2,1)S(1)}, u32[]{:S(2)}, u32[]{:S(2)}) collective-permute-start(bf16[256,768]{1,0:T(8,128)(2,1)S(1)} %pad_maximum_fusion.7), channel_id=1, source_target_pairs={{0,1},{1,0},{2,3},{3,2},{4,5},{5,4},{6,7},{7,6},{8,9},{9,8},{10,11... | collective-permute-start | bytes 1179656 | tf_op jit(solution)/shard_map/ppermute | solution.py:31
  19.3 13.5 %collective-permute-start.2 = (bf16[256,768]{1,0:T(8,128)(2,1)S(1)}, bf16[256,768]{1,0:T(8,128)(2,1)S(1)}, u32[]{:S(2)}, u32[]{:S(2)}) collective-permute-start(bf16[256,768]{1,0:T(8,128)(2,1)S(1)} %pad_maximum_fusion.7), channel_id=1, source_target_pairs={{0,4},{1,5},{2,6},{3,7},{4,8},{5,9},{6,10},{7,11},{8,12},{9,13},{1... | collective-permute-start | bytes 1179656 | tf_op jit(solution)/shard_map/ppermute | solution.py:31
  19.4 13.7 %collective-permute-start.3 = (bf16[256,768]{1,0:T(8,128)(2,1)S(1)}, bf16[256,768]{1,0:T(8,128)(2,1)S(1)}, u32[]{:S(2)}, u32[]{:S(2)}) collective-permute-start(bf16[256,768]{1,0:T(8,128)(2,1)S(1)} %pad_maximum_fusion.7), channel_id=1, source_target_pairs={{0,240},{1,241},{2,242},{3,243},{4,0},{5,1},{6,2},{7,3},{8,4},{9,5... | collective-permute-start | bytes 1179656 | tf_op jit(solution)/shard_map/ppermute | solution.py:31
  23.4 12.4 %copy-start.11 = (bf16[1536,768]{1,0:T(8,128)(2,1)S(1)}, bf16[1536,768]{1,0:T(8,128)(2,1)}, u32[]{:S(2)}) copy-start(bf16[1536,768]{1,0:T(8,128)(2,1)} %pad_maximum_fusion) | copy-start | bytes 7077892
  33.1 10.7 %collective-permute-start.6 = (bf16[256,768]{1,0:T(8,128)(2,1)S(1)}, bf16[256,768]{1,0:T(8,128)(2,1)S(1)}, u32[]{:S(2)}, u32[]{:S(2)}) collective-permute-start(bf16[256,768]{1,0:T(8,128)(2,1)S(1)} %collective-permute-done.2), channel_id=1, source_target_pairs={{0,4},{1,5},{2,6},{3,7},{4,8},{5,9},{6,10},{7,11},{8,12},{9,13},{1... | collective-permute-start | bytes 1179656 | tf_op jit(solution)/shard_map/ppermute | solution.py:31
  33.3 3.2 %collective-permute-start.8 = (bf16[256,768]{1,0:T(8,128)(2,1)S(1)}, bf16[256,768]{1,0:T(8,128)(2,1)S(1)}, u32[]{:S(2)}, u32[]{:S(2)}) collective-permute-start(bf16[256,768]{1,0:T(8,128)(2,1)S(1)} %collective-permute-done.2), channel_id=1, source_target_pairs={{0,1},{1,0},{2,3},{3,2},{4,5},{5,4},{6,7},{7,6},{8,9},{9,8},{10,11... | collective-permute-start | bytes 1179656 | tf_op jit(solution)/shard_map/ppermute | solution.py:31
  33.3 3.5 %collective-permute-start.9 = (bf16[256,768]{1,0:T(8,128)(2,1)S(1)}, bf16[256,768]{1,0:T(8,128)(2,1)S(1)}, u32[]{:S(2)}, u32[]{:S(2)}) collective-permute-start(bf16[256,768]{1,0:T(8,128)(2,1)S(1)} %collective-permute-done.3), channel_id=1, source_target_pairs={{0,1},{1,0},{2,3},{3,2},{4,5},{5,4},{6,7},{7,6},{8,9},{9,8},{10,11... | collective-permute-start | bytes 1179656 | tf_op jit(solution)/shard_map/ppermute | solution.py:31
  33.8 13.1 %collective-permute-start.10 = (bf16[256,768]{1,0:T(8,128)(2,1)S(1)}, bf16[256,768]{1,0:T(8,128)(2,1)S(1)}, u32[]{:S(2)}, u32[]{:S(2)}) collective-permute-start(bf16[256,768]{1,0:T(8,128)(2,1)S(1)} %collective-permute-done.3), channel_id=1, source_target_pairs={{0,240},{1,241},{2,242},{3,243},{4,0},{5,1},{6,2},{7,3},{8,4},{9,5... | collective-permute-start | bytes 1179656 | tf_op jit(solution)/shard_map/ppermute | solution.py:31
  43.8 3.9 %collective-permute-start.7 = (bf16[256,768]{1,0:T(8,128)(2,1)S(1)}, bf16[256,768]{1,0:T(8,128)(2,1)S(1)}, u32[]{:S(2)}, u32[]{:S(2)}) collective-permute-start(bf16[256,768]{1,0:T(8,128)(2,1)S(1)} %collective-permute-done.6), channel_id=1, source_target_pairs={{0,1},{1,0},{2,3},{3,2},{4,5},{5,4},{6,7},{7,6},{8,9},{9,8},{10,11... | collective-permute-start | bytes 1179656 | tf_op jit(solution)/shard_map/ppermute | solution.py:31
  46.9 1.8 %collective-permute-start.11 = (bf16[256,768]{1,0:T(8,128)(2,1)S(1)}, bf16[256,768]{1,0:T(8,128)(2,1)S(1)}, u32[]{:S(2)}, u32[]{:S(2)}) collective-permute-start(bf16[256,768]{1,0:T(8,128)(2,1)S(1)} %collective-permute-done.10), channel_id=1, source_target_pairs={{0,1},{1,0},{2,3},{3,2},{4,5},{5,4},{6,7},{7,6},{8,9},{9,8},{10,11... | collective-permute-start | bytes 1179656 | tf_op jit(solution)/shard_map/ppermute | solution.py:31
  56.0 10.4 %copy-start.5 = (f32[256,768]{1,0:T(8,128)}, f32[256,768]{1,0:T(8,128)S(1)}, u32[]{:S(2)}) copy-start(f32[256,768]{1,0:T(8,128)S(1)} %get-tuple-element.42.own_ref) | copy-start | bytes 2359300
  56.0 10.4 %copy-start.7 = (bf16[256,384]{1,0:T(8,128)(2,1)}, bf16[256,384]{1,0:T(8,128)(2,1)S(1)}, u32[]{:S(2)}) copy-start(bf16[256,384]{1,0:T(8,128)(2,1)S(1)} %get-tuple-element.41.dq_ref) | copy-start | bytes 589828
  56.0 10.4 %copy-start.9 = (bf16[256,384]{1,0:T(8,128)(2,1)}, bf16[256,384]{1,0:T(8,128)(2,1)S(1)}, u32[]{:S(2)}) copy-start(bf16[256,384]{1,0:T(8,128)(2,1)S(1)} %get-tuple-element.40) | copy-start | bytes 589828
  56.1 13.7 %collective-permute-start.13 = (bf16[256,768]{1,0:T(8,128)(2,1)S(1)}, bf16[256,768]{1,0:T(8,128)(2,1)S(1)}, u32[]{:S(2)}, u32[]{:S(2)}) collective-permute-start(bf16[256,768]{1,0:T(8,128)(2,1)S(1)} %get-tuple-element.43.refs_5_), channel_id=1, source_target_pairs={{0,240},{1,241},{2,242},{3,243},{4,0},{5,1},{6,2},{7,3},{8,4},{9,5... | collective-permute-start | bytes 1179656 | tf_op jit(solution)/shard_map/ppermute | solution.py:31
  56.1 14.5 %collective-permute-start.15 = (bf16[256,768]{1,0:T(8,128)(2,1)S(1)}, bf16[256,768]{1,0:T(8,128)(2,1)S(1)}, u32[]{:S(2)}, u32[]{:S(2)}) collective-permute-start(bf16[256,768]{1,0:T(8,128)(2,1)S(1)} %get-tuple-element.47.refs_9_), channel_id=1, source_target_pairs={{0,4},{1,5},{2,6},{3,7},{4,8},{5,9},{6,10},{7,11},{8,12},{9,13},{1... | collective-permute-start | bytes 1179656 | tf_op jit(solution)/shard_map/ppermute | solution.py:31
  66.4 14.3 %copy-start.2 = (bf16[2,4,48,1152]{3,2,1,0:T(8,128)(2,1)S(1)}, bf16[2,4,48,1152]{3,2,1,0:T(8,128)(2,1)}, u32[]{:S(2)}) copy-start(bf16[2,4,48,1152]{3,2,1,0:T(8,128)(2,1)} %get-tuple-element.48.refs_0_) | copy-start | bytes 2654212
  66.5 13.3 %collective-permute-start.12 = (bf16[2,4,48,1152]{3,2,1,0:T(8,128)(2,1)}, bf16[2,4,48,1152]{3,2,1,0:T(8,128)(2,1)S(1)}, u32[]{:S(2)}, u32[]{:S(2)}) collective-permute-start(bf16[2,4,48,1152]{3,2,1,0:T(8,128)(2,1)} %get-tuple-element.49), channel_id=1, source_target_pairs={{0,64},{1,193},{2,66},{3,195},{4,68},{5,197},{6,70},{7,199},{8,72}... | collective-permute-start | bytes 2654216 | tf_op jit(solution)/shard_map/ppermute | solution.py:31
  68.0 25.3 %collective-permute-start.19 = (bf16[2,4,48,1152]{3,2,1,0:T(8,128)(2,1)}, bf16[2,4,48,1152]{3,2,1,0:T(8,128)(2,1)S(1)}, u32[]{:S(2)}, u32[]{:S(2)}) collective-permute-start(bf16[2,4,48,1152]{3,2,1,0:T(8,128)(2,1)} %get-tuple-element.57), channel_id=1, source_target_pairs={{0,16},{1,49},{2,18},{3,51},{4,20},{5,53},{6,22},{7,55},{8,24},{9,... | collective-permute-start | bytes 2654216 | tf_op jit(solution)/shard_map/ppermute | solution.py:31
  70.6 22.7 %copy-start.1 = (bf16[2,4,48,1152]{3,2,1,0:T(8,128)(2,1)S(1)}, bf16[2,4,48,1152]{3,2,1,0:T(8,128)(2,1)}, u32[]{:S(2)}) copy-start(bf16[2,4,48,1152]{3,2,1,0:T(8,128)(2,1)} %get-tuple-element.56.refs_0_) | copy-start | bytes 2654212
  70.6 23.7 %collective-permute-start.14 = (bf16[256,768]{1,0:T(8,128)(2,1)}, bf16[256,768]{1,0:T(8,128)(2,1)}, u32[]{:S(2)}, u32[]{:S(2)}) collective-permute-start(bf16[256,768]{1,0:T(8,128)(2,1)} %add_convert_fusion.2), channel_id=1, source_target_pairs={{0,240},{1,241},{2,242},{3,243},{4,0},{5,1},{6,2},{7,3},{8,4},{9,5... | collective-permute-start | bytes 1179656 | tf_op jit(solution)/shard_map/ppermute | solution.py:31
  71.5 22.9 %collective-permute-start.16 = (bf16[256,768]{1,0:T(8,128)(2,1)}, bf16[256,768]{1,0:T(8,128)(2,1)}, u32[]{:S(2)}, u32[]{:S(2)}) collective-permute-start(bf16[256,768]{1,0:T(8,128)(2,1)} %add_convert_fusion.1), channel_id=1, source_target_pairs={{0,4},{1,5},{2,6},{3,7},{4,8},{5,9},{6,10},{7,11},{8,12},{9,13},{1... | collective-permute-start | bytes 1179656 | tf_op jit(solution)/shard_map/ppermute | solution.py:31
  79.8 0.9 copy-start.3
  80.7 1.2 copy-start.4
  81.9 12.5 %copy-start.6 = (f32[256,768]{1,0:T(8,128)S(1)}, f32[256,768]{1,0:T(8,128)}, u32[]{:S(2)}) copy-start(f32[256,768]{1,0:T(8,128)} %copy-done.5) | copy-start | bytes 2359300
  81.9 12.5 %copy-start.8 = (bf16[256,384]{1,0:T(8,128)(2,1)S(1)}, bf16[256,384]{1,0:T(8,128)(2,1)}, u32[]{:S(2)}) copy-start(bf16[256,384]{1,0:T(8,128)(2,1)} %copy-done.7) | copy-start | bytes 589828
  82.8 17.2 %collective-permute-start.20 = (bf16[4,48,1152]{2,1,0:T(8,128)(2,1)}, bf16[4,48,1152]{2,1,0:T(8,128)(2,1)}, u32[]{:S(2)}, u32[]{:S(2)}) collective-permute-start(bf16[4,48,1152]{2,1,0:T(8,128)(2,1)} %get-tuple-element.50), channel_id=1, source_target_pairs={{0,192},{1,65},{2,194},{3,67},{4,196},{5,69},{6,198},{7,71},{8,200... | collective-permute-start | bytes 1327112 | tf_op jit(solution)/shard_map/ppermute | solution.py:31
  94.3 9.7 %collective-permute-start.21 = (bf16[4,48,1152]{2,1,0:T(8,128)(2,1)}, bf16[4,48,1152]{2,1,0:T(8,128)(2,1)S(1)}, u32[]{:S(2)}, u32[]{:S(2)}) collective-permute-start(bf16[4,48,1152]{2,1,0:T(8,128)(2,1)} %get-tuple-element.59), channel_id=1, source_target_pairs={{0,48},{1,17},{2,50},{3,19},{4,52},{5,21},{6,54},{7,23},{8,56},{9,... | collective-permute-start | bytes 1327112 | tf_op jit(solution)/shard_map/ppermute | solution.py:31
  98.3 7.0 %collective-permute-start.17 = (bf16[2,256,384]{2,1,0:T(8,128)(2,1)S(1)}, bf16[2,256,384]{2,1,0:T(8,128)(2,1)}, u32[]{:S(2)}, u32[]{:S(2)}) collective-permute-start(bf16[2,256,384]{2,1,0:T(8,128)(2,1)S(1)} %get-tuple-element.54), channel_id=1, source_target_pairs={{0,1},{1,0},{2,3},{3,2},{4,5},{5,4},{6,7},{7,6},{8,9},{9,8},{10,11... | collective-permute-start | bytes 1179656 | tf_op jit(solution)/shard_map/ppermute | solution.py:31
  105.2 6.0 %collective-permute-start.22 = (bf16[2,48,1152]{2,1,0:T(8,128)(2,1)S(1)}, bf16[2,48,1152]{2,1,0:T(8,128)(2,1)S(1)}, u32[]{:S(2)}, u32[]{:S(2)}) collective-permute-start(bf16[2,48,1152]{2,1,0:T(8,128)(2,1)S(1)} %get-tuple-element.61), channel_id=1, source_target_pairs={{0,16},{1,49},{2,18},{3,51},{4,20},{5,53},{6,22},{7,55},{8,24},{9,... | collective-permute-start | bytes 663560 | tf_op jit(solution)/shard_map/ppermute | solution.py:31
  105.3 9.1 %copy-start.10 = (bf16[256,384]{1,0:T(8,128)(2,1)S(1)}, bf16[256,384]{1,0:T(8,128)(2,1)}, u32[]{:S(2)}) copy-start(bf16[256,384]{1,0:T(8,128)(2,1)} %copy-done.9) | copy-start | bytes 589828
  106.5 7.0 %collective-permute-start.24 = (bf16[256,384]{1,0:T(8,128)(2,1)S(1)}, bf16[256,384]{1,0:T(8,128)(2,1)S(1)}, u32[]{:S(2)}, u32[]{:S(2)}) collective-permute-start(bf16[256,384]{1,0:T(8,128)(2,1)S(1)} %get-tuple-element.82), channel_id=1, source_target_pairs={{0,2},{1,3},{2,0},{3,1},{4,6},{5,7},{6,4},{7,5},{8,10},{9,11},{10,... | collective-permute-start | bytes 589832 | tf_op jit(solution)/shard_map/ppermute | solution.py:31
  106.6 6.0 %collective-permute-start.23 = (bf16[2,48,1152]{2,1,0:T(8,128)(2,1)S(1)}, bf16[2,48,1152]{2,1,0:T(8,128)(2,1)S(1)}, u32[]{:S(2)}, u32[]{:S(2)}) collective-permute-start(bf16[2,48,1152]{2,1,0:T(8,128)(2,1)S(1)} %get-tuple-element.63), channel_id=1, source_target_pairs={{0,64},{1,193},{2,66},{3,195},{4,68},{5,197},{6,70},{7,199},{8,72}... | collective-permute-start | bytes 663560 | tf_op jit(solution)/shard_map/ppermute | solution.py:31
  113.5 6.8 %collective-permute-start.26 = (bf16[48,1152]{1,0:T(8,128)(2,1)S(1)}, bf16[48,1152]{1,0:T(8,128)(2,1)S(1)}, u32[]{:S(2)}, u32[]{:S(2)}) collective-permute-start(bf16[48,1152]{1,0:T(8,128)(2,1)S(1)} %fusion.8), channel_id=1, source_target_pairs={{0,192},{1,65},{2,194},{3,67},{4,196},{5,69},{6,198},{7,71},{8,200... | collective-permute-start | bytes 331784 | tf_op jit(solution)/shard_map/ppermute | solution.py:31
  114.4 15.6 %collective-permute-start.18 = (bf16[2,256,384]{2,1,0:T(8,128)(2,1)S(1)}, bf16[2,256,384]{2,1,0:T(8,128)(2,1)S(1)}, u32[]{:S(2)}, u32[]{:S(2)}) collective-permute-start(bf16[2,256,384]{2,1,0:T(8,128)(2,1)S(1)} %pad_maximum_fusion.8), channel_id=1, source_target_pairs={{0,0},{1,1},{2,2},{3,3},{4,4},{5,5},{6,6},{7,7},{8,8},{9,9},{10,10... | collective-permute-start | bytes 1179656 | tf_op jit(solution)/shard_map/ppermute | solution.py:31
  120.3 6.0 %collective-permute-start.25 = (bf16[48,1152]{1,0:T(8,128)(2,1)S(1)}, bf16[48,1152]{1,0:T(8,128)(2,1)S(1)}, u32[]{:S(2)}, u32[]{:S(2)}) collective-permute-start(bf16[48,1152]{1,0:T(8,128)(2,1)S(1)} %fusion.7), channel_id=1, source_target_pairs={{0,48},{1,17},{2,50},{3,19},{4,52},{5,21},{6,54},{7,23},{8,56},{9,... | collective-permute-start | bytes 331784 | tf_op jit(solution)/shard_map/ppermute | solution.py:31
  126.4 5.0 %collective-permute-start.29 = (bf16[24,1152]{1,0:T(8,128)(2,1)S(1)}, bf16[24,1152]{1,0:T(8,128)(2,1)S(1)}, u32[]{:S(2)}, u32[]{:S(2)}) collective-permute-start(bf16[24,1152]{1,0:T(8,128)(2,1)S(1)} %get-tuple-element.80), channel_id=1, source_target_pairs={{0,12},{1,13},{2,14},{3,15},{4,0},{5,1},{6,2},{7,3},{8,4},{9,5},{1... | collective-permute-start | bytes 165896 | tf_op jit(solution)/shard_map/ppermute | solution.py:31
  126.5 7.2 %collective-permute-start.28 = (bf16[24,1152]{1,0:T(8,128)(2,1)S(1)}, bf16[24,1152]{1,0:T(8,128)(2,1)S(1)}, u32[]{:S(2)}, u32[]{:S(2)}) collective-permute-start(bf16[24,1152]{1,0:T(8,128)(2,1)S(1)} %get-tuple-element.81), channel_id=1, source_target_pairs={{0,8},{1,9},{2,10},{3,11},{4,12},{5,13},{6,14},{7,15},{8,0},{9,1},... | collective-permute-start | bytes 165896 | tf_op jit(solution)/shard_map/ppermute | solution.py:31
  126.6 7.1 %collective-permute-start.27 = (bf16[24,1152]{1,0:T(8,128)(2,1)S(1)}, bf16[24,1152]{1,0:T(8,128)(2,1)S(1)}, u32[]{:S(2)}, u32[]{:S(2)}) collective-permute-start(bf16[24,1152]{1,0:T(8,128)(2,1)S(1)} %get-tuple-element.79), channel_id=1, source_target_pairs={{0,4},{1,5},{2,6},{3,7},{4,8},{5,9},{6,10},{7,11},{8,12},{9,13},{1... | collective-permute-start | bytes 165896 | tf_op jit(solution)/shard_map/ppermute | solution.py:31
